TPU v7x, 512 devices: a whole 4x8x8 slice. The times are simulated.
512 devices in a mesh: gx: 64 (over y, z_hi, x), gy: 8 (over z_lo, core).
Axes of the slice: x: 4, y: 8, z: 8 (z_hi: 2, z_lo: 4; z = z_hi * 4 + z_lo), core: 2. Of those that a mesh axis runs over, the one named last changes fastest.
Arguments:
- populations: float32 [19, 128, 16, 2048], P(None, 'gx', None, 'gy'), may hold values from 0 to 1
- mass: float32 [128, 16, 2048], P('gx', None, 'gy'), may hold values from 0.05 to 0.95
- flags: int32 [2, 128, 16, 2048], P(None, 'gx', None, 'gy'), may hold values from 0 to 3
- relax: float32 [128, 16, 2048], P('gx', None, 'gy'), may hold values from 0.6 to 1.9
Outputs:
- populations_out: float32 [19, 128, 16, 2048], P(None, 'gx', None, 'gy')
- mass_out: float32 [128, 16, 2048], P('gx', None, 'gy')
Inputs may be any that keep to these rules, and one draw needn't show every extreme that they name: `flags`: 0 gas, 1 interface, 2 liquid, 3 wall.
All inputs are finite; a program needn't handle non-finite values.
Results may differ from a plain program's by a relative error of at most 0.0003.
Values sent between devices are 32-bit elements; how exact they have to be, the bound alone decides.
A program may use at most 64 MiB of HBM per device.

v0:
```python
import jax
import jax.numpy as jnp
import numpy as np
from jax import lax
from jax.sharding import PartitionSpec as P

lattice_list = [
    (0, 0, 0),
    (1, 0, 0),
    (-1, 0, 0),
    (0, 1, 0),
    (0, -1, 0),
    (0, 0, 1),
    (0, 0, -1),
    (1, 1, 0),
    (-1, -1, 0),
    (1, -1, 0),
    (-1, 1, 0),
    (1, 0, 1),
    (-1, 0, -1),
    (1, 0, -1),
    (-1, 0, 1),
    (0, 1, 1),
    (0, -1, -1),
    (0, 1, -1),
    (0, -1, 1),
]
opposite_index = [0, 2, 1, 4, 3, 6, 5, 8, 7, 10, 9, 12, 11, 14, 13, 16, 15, 18, 17]
lattice_weight = np.array([1.0 / 3.0] + [1.0 / 18.0] * 6 + [1.0 / 36.0] * 12, np.float32)
lattice_vel = np.array(lattice_list, np.float32)
pair_table = np.stack(
    [
        lattice_vel[:, 0] ** 2,
        lattice_vel[:, 1] ** 2,
        lattice_vel[:, 2] ** 2,
        2 * lattice_vel[:, 0] * lattice_vel[:, 1],
        2 * lattice_vel[:, 0] * lattice_vel[:, 2],
        2 * lattice_vel[:, 1] * lattice_vel[:, 2],
    ],
    1,
).astype(np.float32)
surface_sigma = 0.02
highest = lax.Precision.HIGHEST


def padded_2(cells, sides, width):
    for axis, dim in sides:
        count = lax.axis_size(axis)
        head = lax.slice_in_dim(cells, 0, width, axis=dim)
        tail = lax.slice_in_dim(cells, cells.shape[dim] - width, cells.shape[dim], axis=dim)
        cells = jnp.concatenate(
            [
                lax.ppermute(tail, axis, [(i, (i + 1) % count) for i in range(count)]),
                cells,
                lax.ppermute(head, axis, [((i + 1) % count, i) for i in range(count)]),
            ],
            axis=dim,
        )
    return cells


def advance(extended, mass, kinds, relax):
    width_x = extended.shape[1] - 2
    depth = extended.shape[2]
    width_y = extended.shape[3] - 2
    padded = jnp.pad(extended, ((0, 0), (0, 0), (1, 1), (0, 0)))
    edge_plane = jnp.zeros(padded.shape[1:], jnp.float32).at[:, 0].set(-1.0).at[:, -1].set(-1.0)
    padded = padded.at[19].add(edge_plane)
    pops = extended[:19, 1:-1, :, 1:-1]
    source_pop = []
    source_code = []
    for index in range(19):
        shift_x, shift_y, shift_z = lattice_list[index]
        source_pop.append(
            padded[
                index,
                1 - shift_x : 1 - shift_x + width_x,
                1 - shift_z : 1 - shift_z + depth,
                1 - shift_y : 1 - shift_y + width_y,
            ]
        )
        source_code.append(
            padded[
                19,
                1 - shift_x : 1 - shift_x + width_x,
                1 - shift_z : 1 - shift_z + depth,
                1 - shift_y : 1 - shift_y + width_y,
            ]
        )
    source_pop = jnp.stack(source_pop)
    source_code = jnp.stack(source_code)
    reverse = jnp.stack([pops[other] for other in opposite_index])
    weights = jnp.asarray(lattice_weight)[:, None, None, None]
    velocity = jnp.asarray(lattice_vel)
    is_face = kinds == 1
    is_liquid = kinds == 2
    is_fluid = is_face | is_liquid
    momentum_old = jnp.tensordot(velocity.T, pops, axes=1, precision=highest)
    own_frac = jnp.where(is_liquid, 1.0, jnp.where(is_face, mass, 0.0))
    near_frac = jnp.where(
        source_code == 1.0, 1.0, jnp.where(source_code > 1.5, source_code - 2.0, 0.0)
    )
    laplace = jnp.sum(near_frac[1:7], 0) - 6.0 * own_frac
    gas_density = 1.0 - 3.0 * surface_sigma * laplace
    proj_old = jnp.tensordot(velocity, momentum_old, axes=1, precision=highest)
    square_old = jnp.sum(momentum_old * momentum_old, 0)
    rebuilt = 2.0 * weights * (gas_density + 4.5 * proj_old * proj_old - 1.5 * square_old) - reverse
    incoming = jnp.where(
        source_code == -1.0, reverse, jnp.where(source_code == 0.0, rebuilt, source_pop)
    )
    share = jnp.where(
        source_code == 1.0,
        1.0,
        jnp.where(source_code > 1.5, 0.5 * (mass + (source_code - 2.0)), 0.0),
    )
    moved_mass = jnp.sum((share * (source_pop - reverse))[1:], 0)
    density = jnp.sum(incoming, 0)
    mass_new = jnp.where(is_face, mass + moved_mass, jnp.where(is_liquid, density, 0.0))
    momentum = jnp.tensordot(velocity.T, incoming, axes=1, precision=highest)
    projected = jnp.tensordot(velocity, momentum, axes=1, precision=highest)
    square = jnp.sum(momentum * momentum, 0)
    equilibrium = weights * (density + 3.0 * projected + 4.5 * projected * projected - 1.5 * square)
    stress = jnp.tensordot(
        jnp.asarray(pair_table).T, incoming - equilibrium, axes=1, precision=highest
    )
    trace_part = stress[0] + stress[1] + stress[2]
    contraction = (
        jnp.tensordot(jnp.asarray(pair_table), stress, axes=1, precision=highest) - trace_part / 3.0
    )
    collided = equilibrium + (1.0 - relax) * 4.5 * weights * contraction
    pops_new = jnp.where(is_fluid, collided, weights * jnp.ones_like(collided))
    return (pops_new, mass_new)


def cell_code(mass, kinds):
    return jnp.where(
        kinds == 3, -1.0, jnp.where(kinds == 0, 0.0, jnp.where(kinds == 2, 1.0, 2.0 + mass))
    ).astype(jnp.float32)


def extend(stacked):
    return padded_2(stacked, (("gx", 1), ("gy", 3)), 1)


def on_device(populations, mass, flags, relax):
    count_steps = flags.shape[0]
    pops = populations
    fill = mass
    for step in range(count_steps):
        kinds = flags[step]
        stacked = jnp.concatenate([pops, cell_code(fill, kinds)[None]], 0)
        extended = extend(stacked)
        pops, fill = advance(extended, fill, kinds, relax)
    return (pops, fill)


def solution(mesh):
    return jax.shard_map(
        on_device,
        mesh=mesh,
        in_specs=(
            P(None, "gx", None, "gy"),
            P("gx", None, "gy"),
            P(None, "gx", None, "gy"),
            P("gx", None, "gy"),
        ),
        out_specs=(P(None, "gx", None, "gy"), P("gx", None, "gy")),
        check_vma=False,
    )
```

profile of v0, /device:TPU:1, one launch (start us, length us, event | category | flops | bytes accessed | tf_op | source)
XLA Modules:
  0.0 169.3 jit_solution(4159089915806548698)
XLA Ops:
  4.5 16.6 %collective-permute-start.1 = (f32[20,1,16,256]{3,0,2,1:T(8,128)S(1)}, f32[20,1,16,256]{3,0,2,1:T(8,128)S(1)}, u32[]{:S(2)}, u32[]{:S(2)}) collective-permute-start(f32[20,1,16,256]{3,0,2,1:T(8,128)S(1)} %get-tuple-element.120), channel_id=1, source_target_pairs={{8,0},{16,8},{24,16},{32,24},{40,32},{48,40},{56,48},{64,56},{72,6... | collective-permute-start | bytes 983048 | tf_op jit(solution)/shard_map/ppermute | solution.py:55
  21.1 1.9 %collective-permute-start = (f32[20,1,16,256]{3,0,2,1:T(8,128)S(1)}, f32[20,1,16,256]{3,0,2,1:T(8,128)S(1)}, u32[]{:S(2)}, u32[]{:S(2)}) collective-permute-start(f32[20,1,16,256]{3,0,2,1:T(8,128)S(1)} %get-tuple-element.121), channel_id=1, source_target_pairs={{0,8},{8,16},{16,24},{24,32},{32,40},{40,48},{48,56},{56,64},{64,7... | collective-permute-start | bytes 983048 | tf_op jit(solution)/shard_map/ppermute | solution.py:53
  23.7 2.1 %multiply_reduce_fusion.3 = (f32[2,16,256]{2,1,0:T(8,128)}, f32[3,2,16,256]{3,0,2,1:T(4,128)}) fusion(f32[19,3,1,1]{0,1,3,2:T(4,128)S(1)} %copy-done.35, f32[19,2,16,256]{3,2,1,0:T(8,128)S(1)} %copy-done), kind=kOutput, calls=%fused_computation.88 | convolution fusion | flops 5644288 | bytes 753892 | tf_op jit(solution)/shard_map/dot_general | solution.py:98
  25.8 8.0 %collective-permute-done.1 = f32[20,1,16,256]{3,0,2,1:T(8,128)S(1)} collective-permute-done((f32[20,1,16,256]{3,0,2,1:T(8,128)S(1)}, f32[20,1,16,256]{3,0,2,1:T(8,128)S(1)}, u32[]{:S(2)}, u32[]{:S(2)}) %collective-permute-start.1) | collective-permute-done | bytes 327712 | tf_op jit(solution)/shard_map/ppermute | solution.py:55
  33.9 14.0 %collective-permute-done = f32[20,1,16,256]{3,0,2,1:T(8,128)S(1)} collective-permute-done((f32[20,1,16,256]{3,0,2,1:T(8,128)S(1)}, f32[20,1,16,256]{3,0,2,1:T(8,128)S(1)}, u32[]{:S(2)}, u32[]{:S(2)}) %collective-permute-start) | collective-permute-done | bytes 327712 | tf_op jit(solution)/shard_map/ppermute | solution.py:53
  49.9 4.1 %collective-permute-start.2 = (f32[20,4,16,1]{0,2,3,1:T(8,128)S(1)}, f32[20,4,16,1]{0,2,3,1:T(8,128)S(1)}, u32[]{:S(2)}, u32[]{:S(2)}) collective-permute-start(f32[20,4,16,1]{0,2,3,1:T(8,128)S(1)} %copy.34), channel_id=1, source_target_pairs={{0,1},{1,2},{2,3},{3,4},{4,5},{5,6},{6,7},{7,0},{8,9},{9,10},{10,1... | collective-permute-start | bytes 15368 | tf_op jit(solution)/shard_map/ppermute | solution.py:53
  54.0 3.0 %collective-permute-start.3 = (f32[20,4,16,1]{0,2,3,1:T(8,128)}, f32[20,4,16,1]{0,2,3,1:T(8,128)S(1)}, u32[]{:S(2)}, u32[]{:S(2)}) collective-permute-start(f32[20,4,16,1]{0,2,3,1:T(8,128)} %copy.35), channel_id=1, source_target_pairs={{1,0},{2,1},{3,2},{4,3},{5,4},{6,5},{7,6},{0,7},{9,8},{10,9},{11,1... | collective-permute-start | bytes 15368 | tf_op jit(solution)/shard_map/ppermute | solution.py:55
  75.4 2.3 %select_maximum_fusion.5 = f32[20,4,18,258]{3,0,2,1:T(8,128)S(1)} fusion(f32[20,4,16,1]{3,0,2,1:T(8,128)S(1)} %copy.37, f32[20,4,16,1]{3,0,2,1:T(8,128)S(1)} %copy.36, f32[20,1,16,256]{3,0,2,1:T(8,128)S(1)} %collective-permute-done.1, f32[20,1,16,256]{3,0,2,1:T(8,128)S(1)} %collective-permute-done, f32[1,2,16,256]{3,0,2,1:T(1,128)S(1)} %copy-done.10, ...), kind=kLoop, calls=%fused_computation.7 | loop fusion | flops 5201280 | bytes 2807040 | tf_op jit(solution)/shard_map/concatenate | solution.py:51
  79.3 1.8 %fusion.58 = (f32[1,2,16,256]{3,0,2,1:T(1,128)}, f32[1,2,16,256]{3,0,2,1:T(1,128)}, f32[1,2,16,256]{3,0,2,1:T(1,128)}, f32[1,2,16,256]{3,0,2,1:T(1,128)}, f32[1,...) fusion(f32[1,4,18,258]{3,0,2,1:T(1,128)S(1)} %slice_add_fusion.3), kind=kLoop, calls=%fused_computation.157 | loop fusion | bytes 1245184 | tf_op jit(solution)/shard_map/slice | solution.py:83
  81.1 3.4 %stack.18 = f32[19,2,16,256]{3,0,2,1:T(8,128)S(1)} concatenate(f32[1,2,16,256]{3,0,2,1:T(1,128)} %get-tuple-element.201, f32[1,2,16,256]{3,0,2,1:T(1,128)} %get-tuple-element.200, f32[1,2,16,256]{3,0,2,1:T(1,128)} %get-tuple-element.199, f32[1,2,16,256]{3,0,2,1:T(1,128)} %get-tuple-element.198, f32[1,2,16,256]{3,0,2,1:T(1,128)} %get-tuple-element.197, ...), dimensions={0} | concatenate | bytes 1245184 | tf_op jit(solution)/shard_map/stack | solution.py:91
  88.5 3.5 %stack.20 = f32[19,2,16,256]{3,0,2,1:T(8,128)S(1)} concatenate(f32[1,2,16,256]{3,0,2,1:T(1,128)} %get-tuple-element.145, f32[1,2,16,256]{3,0,2,1:T(1,128)} %get-tuple-element.116, f32[1,2,16,256]{3,0,2,1:T(1,128)} %get-tuple-element.117, f32[1,2,16,256]{3,0,2,1:T(1,128)} %get-tuple-element.105, f32[1,2,16,256]{3,0,2,1:T(1,128)} %get-tuple-element.108, ...), dimensions={0} | concatenate | bytes 1245184 | tf_op jit(solution)/shard_map/stack | solution.py:90
  92.0 3.4 %stack.19 = f32[19,2,16,256]{3,0,2,1:T(8,128)S(1)} concatenate(f32[1,2,16,256]{3,0,2,1:T(1,128)} %get-tuple-element.145, f32[1,2,16,256]{3,0,2,1:T(1,128)} %copy.39, f32[1,2,16,256]{3,0,2,1:T(1,128)} %copy.40, f32[1,2,16,256]{3,0,2,1:T(1,128)} %copy.41, f32[1,2,16,256]{3,0,2,1:T(1,128)} %copy.42, f32[1,2,16,256]{3,0,2,1:T(1,128)} %copy.43, f32[1,2,16,256]{3,0,2,1:T(1,128)} %copy.44, ...), dimensions={0} | concatenate | bytes 1245184 | tf_op jit(solution)/shard_map/stack | solution.py:92
  95.5 1.6 fusion.33
  102.4 1.9 %collective-permute-start.5 = (f32[20,1,16,256]{3,0,2,1:T(8,128)S(1)}, f32[20,1,16,256]{3,0,2,1:T(8,128)S(1)}, u32[]{:S(2)}, u32[]{:S(2)}) collective-permute-start(f32[20,1,16,256]{3,0,2,1:T(8,128)S(1)} %get-tuple-element.118), channel_id=1, source_target_pairs={{8,0},{16,8},{24,16},{32,24},{40,32},{48,40},{56,48},{64,56},{72,6... | collective-permute-start | bytes 983048 | tf_op jit(solution)/shard_map/ppermute | solution.py:55
  104.3 3.6 %collective-permute-start.4 = (f32[20,1,16,256]{3,0,2,1:T(8,128)S(1)}, f32[20,1,16,256]{3,0,2,1:T(8,128)S(1)}, u32[]{:S(2)}, u32[]{:S(2)}) collective-permute-start(f32[20,1,16,256]{3,0,2,1:T(8,128)S(1)} %get-tuple-element.119), channel_id=1, source_target_pairs={{0,8},{8,16},{16,24},{24,32},{32,40},{40,48},{48,56},{56,64},{64,7... | collective-permute-start | bytes 983048 | tf_op jit(solution)/shard_map/ppermute | solution.py:53
  111.4 14.2 %collective-permute-done.4 = f32[20,1,16,256]{3,0,2,1:T(8,128)S(1)} collective-permute-done((f32[20,1,16,256]{3,0,2,1:T(8,128)S(1)}, f32[20,1,16,256]{3,0,2,1:T(8,128)S(1)}, u32[]{:S(2)}, u32[]{:S(2)}) %collective-permute-start.4) | collective-permute-done | bytes 327712 | tf_op jit(solution)/shard_map/ppermute | solution.py:53
  126.9 8.5 %collective-permute-start.6 = (f32[20,4,16,1]{0,2,3,1:T(8,128)S(1)}, f32[20,4,16,1]{0,2,3,1:T(8,128)S(1)}, u32[]{:S(2)}, u32[]{:S(2)}) collective-permute-start(f32[20,4,16,1]{0,2,3,1:T(8,128)S(1)} %copy.60), channel_id=1, source_target_pairs={{0,1},{1,2},{2,3},{3,4},{4,5},{5,6},{6,7},{7,0},{8,9},{9,10},{10,1... | collective-permute-start | bytes 15368 | tf_op jit(solution)/shard_map/ppermute | solution.py:53
  135.4 3.7 %collective-permute-start.7 = (f32[20,4,16,1]{0,2,3,1:T(8,128)S(1)}, f32[20,4,16,1]{0,2,3,1:T(8,128)S(1)}, u32[]{:S(2)}, u32[]{:S(2)}) collective-permute-start(f32[20,4,16,1]{0,2,3,1:T(8,128)S(1)} %copy.61), channel_id=1, source_target_pairs={{1,0},{2,1},{3,2},{4,3},{5,4},{6,5},{7,6},{0,7},{9,8},{10,9},{11,1... | collective-permute-start | bytes 15368 | tf_op jit(solution)/shard_map/ppermute | solution.py:55
  141.7 2.1 %select_maximum_fusion = f32[20,4,18,258]{3,0,2,1:T(8,128)S(1)} fusion(f32[20,4,16,1]{3,0,2,1:T(8,128)S(1)} %copy.63, f32[20,4,16,1]{3,0,2,1:T(8,128)S(1)} %copy.62, f32[20,1,16,256]{3,0,2,1:T(8,128)S(1)} %collective-permute-done.5, f32[20,1,16,256]{3,0,2,1:T(8,128)S(1)} %collective-permute-done.4, f32[1,2,16,256]{3,0,2,1:T(1,128)S(1)} %broadcast_in_dim.65, ...), kind=kLoop, calls=%fused_computation.2 | loop fusion | flops 5201280 | bytes 2807040 | tf_op jit(solution)/shard_map/concatenate | solution.py:51
  145.3 1.8 %fusion.57 = (f32[1,2,16,256]{3,0,2,1:T(1,128)}, f32[1,2,16,256]{3,0,2,1:T(1,128)}, f32[1,2,16,256]{3,0,2,1:T(1,128)}, f32[1,2,16,256]{3,0,2,1:T(1,128)}, f32[1,...) fusion(f32[1,4,18,258]{3,0,2,1:T(1,128)S(1)} %slice_add_fusion.2), kind=kLoop, calls=%fused_computation.156 | loop fusion | bytes 1245184 | tf_op jit(solution)/shard_map/slice | solution.py:83
  147.2 3.4 %stack.21 = f32[19,2,16,256]{3,0,2,1:T(8,128)S(1)} concatenate(f32[1,2,16,256]{3,0,2,1:T(1,128)} %get-tuple-element.182, f32[1,2,16,256]{3,0,2,1:T(1,128)} %get-tuple-element.181, f32[1,2,16,256]{3,0,2,1:T(1,128)} %get-tuple-element.180, f32[1,2,16,256]{3,0,2,1:T(1,128)} %get-tuple-element.179, f32[1,2,16,256]{3,0,2,1:T(1,128)} %get-tuple-element.178, ...), dimensions={0} | concatenate | bytes 1245184 | tf_op jit(solution)/shard_map/stack | solution.py:91
  154.6 3.5 %stack.23 = f32[19,2,16,256]{3,0,2,1:T(8,128)S(1)} concatenate(f32[1,2,16,256]{3,0,2,1:T(1,128)} %get-tuple-element.142, f32[1,2,16,256]{3,0,2,1:T(1,128)} %get-tuple-element.114, f32[1,2,16,256]{3,0,2,1:T(1,128)} %get-tuple-element.115, f32[1,2,16,256]{3,0,2,1:T(1,128)} %get-tuple-element.99, f32[1,2,16,256]{3,0,2,1:T(1,128)} %get-tuple-element.102, ...), dimensions={0} | concatenate | bytes 1245184 | tf_op jit(solution)/shard_map/stack | solution.py:90
  158.0 3.4 %stack.22 = f32[19,2,16,256]{3,0,2,1:T(8,128)S(1)} concatenate(f32[1,2,16,256]{3,0,2,1:T(1,128)} %get-tuple-element.142, f32[1,2,16,256]{3,0,2,1:T(1,128)} %get-tuple-element.141, f32[1,2,16,256]{3,0,2,1:T(1,128)} %get-tuple-element.140, f32[1,2,16,256]{3,0,2,1:T(1,128)} %get-tuple-element.139, f32[1,2,16,256]{3,0,2,1:T(1,128)} %get-tuple-element.138, ...), dimensions={0} | concatenate | bytes 1245184 | tf_op jit(solution)/shard_map/stack | solution.py:92
  161.5 1.6 fusion.28
  (178 shorter events, 54.1 us)
Async XLA Ops:
  0.6 23.1 %copy-start.35 = (f32[19,3,1,1]{0,1,3,2:T(4,128)S(1)}, f32[19,3,1,1]{0,1,3,2:T(4,128)}, u32[]{:S(2)}) copy-start(f32[19,3,1,1]{0,1,3,2:T(4,128)} %constant.201) | copy-start | bytes 688
  0.6 22.4 %copy-start = (f32[19,2,16,256]{3,2,1,0:T(8,128)S(1)}, f32[19,2,16,256]{3,2,1,0:T(8,128)}, u32[]{:S(2)}) copy-start(f32[19,2,16,256]{3,2,1,0:T(8,128)} %param.19) | copy-start | bytes 1867780
  3.0 45.1 %copy-start.9 = (f32[1,2,16,256]{3,0,2,1:T(1,128)}, f32[1,2,16,256]{3,0,2,1:T(1,128)S(1)}, u32[]{:S(2)}) copy-start(f32[1,2,16,256]{3,0,2,1:T(1,128)S(1)} %copy.33) | copy-start | bytes 98308
  4.5 29.3 %collective-permute-start.1 = (f32[20,1,16,256]{3,0,2,1:T(8,128)S(1)}, f32[20,1,16,256]{3,0,2,1:T(8,128)S(1)}, u32[]{:S(2)}, u32[]{:S(2)}) collective-permute-start(f32[20,1,16,256]{3,0,2,1:T(8,128)S(1)} %get-tuple-element.120), channel_id=1, source_target_pairs={{8,0},{16,8},{24,16},{32,24},{40,32},{48,40},{56,48},{64,56},{72,6... | collective-permute-start | bytes 983048 | tf_op jit(solution)/shard_map/ppermute | solution.py:55
  21.1 26.8 %collective-permute-start = (f32[20,1,16,256]{3,0,2,1:T(8,128)S(1)}, f32[20,1,16,256]{3,0,2,1:T(8,128)S(1)}, u32[]{:S(2)}, u32[]{:S(2)}) collective-permute-start(f32[20,1,16,256]{3,0,2,1:T(8,128)S(1)} %get-tuple-element.121), channel_id=1, source_target_pairs={{0,8},{8,16},{16,24},{24,32},{32,40},{40,48},{48,56},{56,64},{64,7... | collective-permute-start | bytes 983048 | tf_op jit(solution)/shard_map/ppermute | solution.py:53
  47.9 27.5 %copy-start.1 = (f32[20,1,16,256]{3,0,2,1:T(8,128)}, f32[20,1,16,256]{3,0,2,1:T(8,128)S(1)}, u32[]{:S(2)}) copy-start(f32[20,1,16,256]{3,0,2,1:T(8,128)S(1)} %collective-permute-done) | copy-start | bytes 983044
  49.9 25.5 %copy-start.10 = (f32[1,2,16,256]{3,0,2,1:T(1,128)S(1)}, f32[1,2,16,256]{3,0,2,1:T(1,128)}, u32[]{:S(2)}) copy-start(f32[1,2,16,256]{3,0,2,1:T(1,128)} %copy-done.9) | copy-start | bytes 98308
  49.9 25.0 %collective-permute-start.2 = (f32[20,4,16,1]{0,2,3,1:T(8,128)S(1)}, f32[20,4,16,1]{0,2,3,1:T(8,128)S(1)}, u32[]{:S(2)}, u32[]{:S(2)}) collective-permute-start(f32[20,4,16,1]{0,2,3,1:T(8,128)S(1)} %copy.34), channel_id=1, source_target_pairs={{0,1},{1,2},{2,3},{3,4},{4,5},{5,6},{6,7},{7,0},{8,9},{9,10},{10,1... | collective-permute-start | bytes 15368 | tf_op jit(solution)/shard_map/ppermute | solution.py:53
  54.0 20.4 %collective-permute-start.3 = (f32[20,4,16,1]{0,2,3,1:T(8,128)}, f32[20,4,16,1]{0,2,3,1:T(8,128)S(1)}, u32[]{:S(2)}, u32[]{:S(2)}) collective-permute-start(f32[20,4,16,1]{0,2,3,1:T(8,128)} %copy.35), channel_id=1, source_target_pairs={{1,0},{2,1},{3,2},{4,3},{5,4},{6,5},{7,6},{0,7},{9,8},{10,9},{11,1... | collective-permute-start | bytes 15368 | tf_op jit(solution)/shard_map/ppermute | solution.py:55
  75.4 3.7 %copy-start.26 = (f32[1,4,18,258]{3,0,2,1:T(1,128)S(1)}, f32[1,4,18,258]{3,0,2,1:T(1,128)}, u32[]{:S(2)}) copy-start(f32[1,4,18,258]{3,0,2,1:T(1,128)} %constant.180.clone.1) | copy-start | bytes 222916
  88.5 6.9 %copy-start.8 = (f32[19,2,16,256]{3,0,2,1:T(8,128)S(1)}, f32[19,2,16,256]{3,0,2,1:T(8,128)}, u32[]{:S(2)}) copy-start(f32[19,2,16,256]{3,0,2,1:T(8,128)} %copy-done.7) | copy-start | bytes 1867780
  88.5 7.0 %copy-start.19 = (pred[19,2,16,256]{3,0,2,1:T(8,128)(4,1)S(1)}, pred[19,2,16,256]{3,0,2,1:T(8,128)(4,1)}, u32[]{:S(2)}) copy-start(pred[19,2,16,256]{3,0,2,1:T(8,128)(4,1)} %copy-done.18) | copy-start | bytes 466948
  88.5 7.0 %copy-start.21 = (pred[19,2,16,256]{3,0,2,1:T(8,128)(4,1)S(1)}, pred[19,2,16,256]{3,0,2,1:T(8,128)(4,1)}, u32[]{:S(2)}) copy-start(pred[19,2,16,256]{3,0,2,1:T(8,128)(4,1)} %copy-done.20) | copy-start | bytes 466948
  99.1 42.6 %copy-start.12 = (f32[1,2,16,256]{3,0,2,1:T(1,128)}, f32[1,2,16,256]{3,0,2,1:T(1,128)S(1)}, u32[]{:S(2)}) copy-start(f32[1,2,16,256]{3,0,2,1:T(1,128)S(1)} %broadcast_in_dim.65) | copy-start | bytes 98308
  102.4 9.0 %collective-permute-start.5 = (f32[20,1,16,256]{3,0,2,1:T(8,128)S(1)}, f32[20,1,16,256]{3,0,2,1:T(8,128)S(1)}, u32[]{:S(2)}, u32[]{:S(2)}) collective-permute-start(f32[20,1,16,256]{3,0,2,1:T(8,128)S(1)} %get-tuple-element.118), channel_id=1, source_target_pairs={{8,0},{16,8},{24,16},{32,24},{40,32},{48,40},{56,48},{64,56},{72,6... | collective-permute-start | bytes 983048 | tf_op jit(solution)/shard_map/ppermute | solution.py:55
  104.3 21.2 %collective-permute-start.4 = (f32[20,1,16,256]{3,0,2,1:T(8,128)S(1)}, f32[20,1,16,256]{3,0,2,1:T(8,128)S(1)}, u32[]{:S(2)}, u32[]{:S(2)}) collective-permute-start(f32[20,1,16,256]{3,0,2,1:T(8,128)S(1)} %get-tuple-element.119), channel_id=1, source_target_pairs={{0,8},{8,16},{16,24},{24,32},{32,40},{40,48},{48,56},{56,64},{64,7... | collective-permute-start | bytes 983048 | tf_op jit(solution)/shard_map/ppermute | solution.py:53
  125.5 16.1 %copy-start.3 = (f32[20,1,16,256]{3,0,2,1:T(8,128)}, f32[20,1,16,256]{3,0,2,1:T(8,128)S(1)}, u32[]{:S(2)}) copy-start(f32[20,1,16,256]{3,0,2,1:T(8,128)S(1)} %collective-permute-done.4) | copy-start | bytes 983044
  126.9 14.3 %collective-permute-start.6 = (f32[20,4,16,1]{0,2,3,1:T(8,128)S(1)}, f32[20,4,16,1]{0,2,3,1:T(8,128)S(1)}, u32[]{:S(2)}, u32[]{:S(2)}) collective-permute-start(f32[20,4,16,1]{0,2,3,1:T(8,128)S(1)} %copy.60), channel_id=1, source_target_pairs={{0,1},{1,2},{2,3},{3,4},{4,5},{5,6},{6,7},{7,0},{8,9},{9,10},{10,1... | collective-permute-start | bytes 15368 | tf_op jit(solution)/shard_map/ppermute | solution.py:53
  135.4 5.2 %collective-permute-start.7 = (f32[20,4,16,1]{0,2,3,1:T(8,128)S(1)}, f32[20,4,16,1]{0,2,3,1:T(8,128)S(1)}, u32[]{:S(2)}, u32[]{:S(2)}) collective-permute-start(f32[20,4,16,1]{0,2,3,1:T(8,128)S(1)} %copy.61), channel_id=1, source_target_pairs={{1,0},{2,1},{3,2},{4,3},{5,4},{6,5},{7,6},{0,7},{9,8},{10,9},{11,1... | collective-permute-start | bytes 15368 | tf_op jit(solution)/shard_map/ppermute | solution.py:55
  153.6 7.9 %copy-start.6 = (f32[19,2,16,256]{3,0,2,1:T(8,128)S(1)}, f32[19,2,16,256]{3,0,2,1:T(8,128)}, u32[]{:S(2)}) copy-start(f32[19,2,16,256]{3,0,2,1:T(8,128)} %copy-done.5) | copy-start | bytes 1867780
  154.6 7.0 %copy-start.15 = (pred[19,2,16,256]{3,0,2,1:T(8,128)(4,1)S(1)}, pred[19,2,16,256]{3,0,2,1:T(8,128)(4,1)}, u32[]{:S(2)}) copy-start(pred[19,2,16,256]{3,0,2,1:T(8,128)(4,1)} %copy-done.14) | copy-start | bytes 466948
  154.6 7.0 %copy-start.17 = (pred[19,2,16,256]{3,0,2,1:T(8,128)(4,1)S(1)}, pred[19,2,16,256]{3,0,2,1:T(8,128)(4,1)}, u32[]{:S(2)}) copy-start(pred[19,2,16,256]{3,0,2,1:T(8,128)(4,1)} %copy-done.16) | copy-start | bytes 466948
  154.6 8.6 %copy-start.37 = (f32[19,3,1,1]{0,1,3,2:T(4,128)S(1)}, f32[19,3,1,1]{0,1,3,2:T(4,128)}, u32[]{:S(2)}) copy-start(f32[19,3,1,1]{0,1,3,2:T(4,128)} %constant.201) | copy-start | bytes 688
  154.6 8.6 %copy-start.47 = (f32[19]{0:T(128)S(1)}, f32[19]{0:T(128)}, u32[]{:S(2)}) copy-start(f32[19]{0:T(128)} %constant.200) | copy-start | bytes 232
  (32 other events, 62.1 us)
where the time goes:
time: 172 us; the launch traced here: 169 us
  local copies, waits for them, and re-layouts  54.5 us (32%)
  starting transfers between devices  43.4 us (25%)
  waiting for transfers between devices  38.2 us (22%)
  other arithmetic  20 us (12%)
  matrix products  11.7 us (7%)
    ppermute x4, waiting for transfers between devices, padded_2(): lax.ppermute(tail, axis, [(i, (i + 1) % count) for i in range(count)])  28.2 us
    ppermute x4, starting transfers between devices, padded_2(): lax.ppermute(head, axis, [((i + 1) % count, i) for i in range(count)])  25.3 us
    ppermute x4, starting transfers between devices, padded_2(): lax.ppermute(tail, axis, [(i, (i + 1) % count) for i in range(count)])  18.1 us
    slice x20, local copies, waits for them, and re-layouts, advance(): reverse = jnp.stack([pops[other] for other in opposite_index])  17.8 us
    ppermute x4, waiting for transfers between devices, padded_2(): lax.ppermute(head, axis, [((i + 1) % count, i) for i in range(count)])  9.99 us
    concatenate x8, other arithmetic, padded_2(): jnp.concatenate([lax.ppermute(tail, axis, [(i, (i + 1) % count) for i in...  8.55 us
    another operation x2, local copies, waits for them, and re-layouts, advance(): source_pop = jnp.stack(source_pop)  6.97 us
    another operation x2, local copies, waits for them, and re-layouts, advance(): reverse = jnp.stack([pops[other] for other in opposite_index])  6.84 us
  transfers between devices with their start and end apart: 8, of which 5 were waited for; matrix products, arithmetic and copies ran while one was open for 14% of the time, Pallas kernels for 0%

commit v1 on v0

v1 whole, which is shorter than its diff:
```python
import jax
import jax.numpy as jnp
from jax import lax
from jax.experimental import pallas as pl
from jax.experimental.pallas import tpu as pltpu
from jax.sharding import PartitionSpec as P

MESH = pl.DeviceIdType.MESH

VEL = [
    (0, 0, 0),
    (1, 0, 0),
    (-1, 0, 0),
    (0, 1, 0),
    (0, -1, 0),
    (0, 0, 1),
    (0, 0, -1),
    (1, 1, 0),
    (-1, -1, 0),
    (1, -1, 0),
    (-1, 1, 0),
    (1, 0, 1),
    (-1, 0, -1),
    (1, 0, -1),
    (-1, 0, 1),
    (0, 1, 1),
    (0, -1, -1),
    (0, 1, -1),
    (0, -1, 1),
]
INDEX = {c: q for q, c in enumerate(VEL)}
OPP = [INDEX[(-a, -b, -c)] for a, b, c in VEL]
W0, W1, W2 = 1.0 / 3.0, 1.0 / 18.0, 1.0 / 36.0
WEIGHT = [W0] + [W1] * 6 + [W2] * 12
SIGMA = 0.02
OFFS = [(0, 0), (1, 0), (-1, 0), (0, 1), (0, -1)]
LANES = 128


def side_dirs(cx):
    return [INDEX[(cx, b, c)] for b, c in OFFS]


def y_columns(cy):
    cols = []
    for plane in (0, 1):
        for cz in (0, 1, -1):
            cols.append((INDEX[(0, cy, cz)], plane))
        cols.append((INDEX[(1 - 2 * plane, cy, 0)], plane))
        cols.append((None, plane))
    return cols


def frac_of(e):
    return jnp.where(e == 1.0, 1.0, jnp.where(e > 1.5, e - 2.0, 0.0))


def code_of(kind, mass):
    return jnp.where(kind == 3, -1.0, jnp.where(kind == 0, 0.0, jnp.where(kind == 2, 1.0, 2.0 + mass)))


def half(h):
    return slice(h * LANES, (h + 1) * LANES)


def shift_y(halves, cy, column):
    lane = lax.broadcasted_iota(jnp.int32, halves[0].shape, 1)
    if cy == 1:
        moved = [pltpu.roll(a, 1, 1) for a in halves]
        edge = lane == 0
        return [jnp.where(edge, column, moved[0]), jnp.where(edge, moved[0], moved[1])]
    moved = [pltpu.roll(a, LANES - 1, 1) for a in halves]
    edge = lane == LANES - 1
    return [jnp.where(edge, moved[1], moved[0]), jnp.where(edge, column, moved[1])]


def shift_z(halves, cz):
    depth = halves[0].shape[0]
    return [pltpu.roll(a, cz % depth, 0) for a in halves]


def wall_z(halves, cz):
    row = lax.broadcasted_iota(jnp.int32, halves[0].shape, 0)
    outside = row == (0 if cz == 1 else halves[0].shape[0] - 1)
    return [jnp.where(outside, -1.0, a) for a in shift_z(halves, cz)]


def spread(tile, k):
    return jnp.broadcast_to(tile[:, k : k + 1], tile.shape)


def pack(columns):
    lane = lax.broadcasted_iota(jnp.int32, (columns[0].shape[0], LANES), 1)
    tile = jnp.zeros(lane.shape, jnp.float32)
    for k, column in enumerate(columns):
        tile = jnp.where(lane == k, jnp.broadcast_to(column, lane.shape), tile)
    return tile


def kernel(
    pops_in,
    mass_in,
    flags_in,
    relax_in,
    pops_out,
    mass_out,
    pops,
    mass,
    flags,
    relax,
    code,
    src,
    near,
    far,
    part,
    sx,
    rx,
    sc,
    rc,
    sy,
    ry,
    sk,
    rk,
    load_sem,
    sx_sem,
    rx_sem,
    sc_sem,
    rc_sem,
    sy_sem,
    ry_sem,
    sk_sem,
    rk_sem,
):
    nx, ny = lax.axis_size("gx"), lax.axis_size("gy")
    gx, gy = lax.axis_index("gx"), lax.axis_index("gy")
    left, right = lax.rem(gx + nx - 1, nx), lax.rem(gx + 1, nx)
    down, up = lax.rem(gy + ny - 1, ny), lax.rem(gy + 1, ny)
    side_id = [(left, gy), (right, gy)]
    y_id = [(gx, down), (gx, up)]
    corner_id = [[(left, down), (left, up)], [(right, down), (right, up)]]

    loads = [
        pltpu.make_async_copy(mass_in, mass.at[0], load_sem.at[0]),
        pltpu.make_async_copy(flags_in, flags, load_sem.at[1]),
        pltpu.make_async_copy(pops_in, pops.at[0], load_sem.at[2]),
        pltpu.make_async_copy(relax_in, relax, load_sem.at[3]),
    ]
    for load in loads:
        load.start()
    barrier = pltpu.get_barrier_semaphore()
    for other in side_id + y_id + corner_id[0] + corner_id[1]:
        pl.semaphore_signal(barrier, inc=1, device_id=other, device_id_type=MESH)

    def send_code(t, d):
        return pltpu.make_async_remote_copy(
            sc.at[t, d], rc.at[t, 1 - d], sc_sem.at[t, d], rc_sem.at[t, 1 - d], device_id=side_id[d], device_id_type=MESH
        )

    def send_pops(t, d, h):
        return pltpu.make_async_remote_copy(
            sx.at[t, d, h],
            rx.at[t, 1 - d, h],
            sx_sem.at[t, d, h],
            rx_sem.at[t, 1 - d, h],
            device_id=side_id[d],
            device_id_type=MESH,
        )

    def send_y(t, u):
        return pltpu.make_async_remote_copy(
            sy.at[t, u], ry.at[t, 1 - u], sy_sem.at[t, u], ry_sem.at[t, 1 - u], device_id=y_id[u], device_id_type=MESH
        )

    def send_corner(t, d, u):
        return pltpu.make_async_remote_copy(
            sk.at[t, d, u],
            rk.at[t, 1 - d, 1 - u],
            sk_sem.at[t, d, u],
            rk_sem.at[t, 1 - d, 1 - u],
            device_id=corner_id[d][u],
            device_id_type=MESH,
        )

    def plane_of(t, q, p):
        return [pops[t, q, p, :, half(h)] for h in (0, 1)]

    def rim(t, q, p, u):
        at = 0 if u == 0 else 2 * LANES - 1
        if q is None:
            return code[t, p, :, at : at + 1]
        return pops[t, q, p, :, at : at + 1]

    def fill_y(t):
        for u in (0, 1):
            sy[t, u] = pack([rim(t, q, p, u) for q, p in y_columns(2 * u - 1)])

    def fill_corner(t, d):
        for u in (0, 1):
            q = INDEX[(2 * d - 1, 2 * u - 1, 0)]
            sk[t, d, u] = pack([rim(t, q, d, u), rim(t, None, d, u)])

    loads[0].wait()
    loads[1].wait()
    for p in (0, 1):
        code[0, p] = code_of(flags[0, p], mass[0, p])
        sc[0, p] = code[0, p]
    loads[2].wait()
    for d in (0, 1):
        fill_corner(0, d)
        for k, q in enumerate(side_dirs(2 * d - 1)):
            cy, cz = OFFS[k]
            halves = plane_of(0, q, d)
            if cy:
                halves = shift_y(halves, cy, halves[0])
            if cz:
                halves = shift_z(halves, cz)
            for h in (0, 1):
                sx[0, d, h, k] = halves[h]
    fill_y(0)
    loads[3].wait()

    pl.semaphore_wait(barrier, 8)
    for d in (0, 1):
        send_code(0, d).start()
    for h in (0, 1):
        for d in (0, 1):
            send_pops(0, d, h).start()
    for d in (0, 1):
        for u in (0, 1):
            send_corner(0, d, u).start()
    for u in (0, 1):
        send_y(0, u).start()

    def stream(t):
        cols = [ry[t, 0], ry[t, 1]]
        place = [{c: k for k, c in enumerate(y_columns(cy))} for cy in (1, -1)]

        def column(q, p, cy):
            u = 0 if cy == 1 else 1
            return spread(cols[u], place[u][(q, p)])

        for p in (0, 1):
            own = [code[t, p, :, half(h)] for h in (0, 1)]
            table = {(0, 0): own}
            for cy in (1, -1):
                table[(cy, 0)] = shift_y(own, cy, column(None, p, cy))
            for cy in (0, 1, -1):
                for cz in (1, -1):
                    table[(cy, cz)] = wall_z(table[(cy, 0)], cz)
            for (cy, cz), halves in table.items():
                for h in (0, 1):
                    near[p, cy + 1, cz + 1, :, half(h)] = halves[h]
            for q, (cx, cy, cz) in enumerate(VEL):
                if q == 0 or not 0 <= p + cx <= 1:
                    continue
                halves = plane_of(t, q, p)
                if cy:
                    halves = shift_y(halves, cy, column(q, p, cy))
                if cz:
                    halves = shift_z(halves, cz)
                for h in (0, 1):
                    src[p + cx, q, :, half(h)] = halves[h]

    def far_codes(t, d):
        own = [rc[t, d, :, half(h)] for h in (0, 1)]
        for k, (cy, cz) in enumerate(OFFS):
            halves = own
            if cy:
                halves = shift_y(own, cy, spread(rk[t, d, 0 if cy == 1 else 1], 1))
            if cz:
                halves = wall_z(own, cz)
            for h in (0, 1):
                far[d, k, :, half(h)] = halves[h]

    def far_sources(t, d, h):
        if t == 0:
            out = [rx[t, d, h, k] for k in range(5)]
            lane = lax.broadcasted_iota(jnp.int32, out[0].shape, 1)
            k, edge, u = (1, lane == 0, 0) if h == 0 else (2, lane == LANES - 1, 1)
            out[k] = jnp.where(edge, spread(rk[t, d, u], 0), out[k])
            return out
        out = []
        for k, (cy, cz) in enumerate(OFFS):
            halves = [rx[t, d, 0, k], rx[t, d, 1, k]]
            if cy:
                halves = shift_y(halves, cy, spread(rk[t, d, 0 if cy == 1 else 1], 0))
            if cz:
                halves = shift_z(halves, cz)
            out.append(halves[h])
        return out

    def arrive(e, s, r, rebuilt, m):
        g = jnp.where(e == -1.0, r, jnp.where(e == 0.0, rebuilt - r, s))
        a = jnp.where(e == 1.0, 1.0, jnp.where(e > 1.5, 0.5 * (m + (e - 2.0)), 0.0))
        return g, a * (s - r)

    def side_moments(cx, g):
        total = (g[0] + g[1]) + (g[2] + (g[3] + g[4]))
        dy, dz, sy2, sz2 = g[1] - g[2], g[3] - g[4], g[1] + g[2], g[3] + g[4]
        if cx == 1:
            return [total, total, dy, dz, total, sy2, sz2, dy, dz]
        return [total, -total, dy, dz, total, sy2, sz2, -dy, -dz]

    def interior(t, p, h):
        ys = half(h)
        kind, m = flags[t, p, :, ys], mass[t, p, :, ys]
        f = [pops[t, q, p, :, ys] for q in range(19)]
        j0 = []
        for axis in range(3):
            plus = [f[q] for q in range(19) if VEL[q][axis] == 1]
            minus = [f[q] for q in range(19) if VEL[q][axis] == -1]
            j0.append(sum(a - b for a, b in zip(plus, minus)))
        own = jnp.where(kind == 2, 1.0, jnp.where(kind == 1, m, 0.0))
        x_far = far[p, 0, :, ys]
        x_near = near[1 - p, 1, 1, :, ys]
        around = frac_of(x_far) + frac_of(x_near)
        for cy, cz in OFFS[1:]:
            around = around + frac_of(near[p, cy + 1, cz + 1, :, ys])
        gas = 1.0 - 3.0 * SIGMA * (around - 6.0 * own)
        lift = 2.0 * gas - 3.0 * (j0[0] * j0[0] + j0[1] * j0[1] + j0[2] * j0[2])

        def rebuilt(q):
            along = [c * j for c, j in zip(VEL[q], j0) if c]
            proj = None
            for c, j in zip(VEL[q], j0):
                if c:
                    term = j if c == 1 else -j
                    proj = term if proj is None else proj + term
            return WEIGHT[q] * (lift + 9.0 * (proj * proj) if along else lift)

        dm = jnp.zeros_like(m)
        g = {}
        e0 = near[p, 1, 1, :, ys]
        g[0] = jnp.where(e0 == 0.0, rebuilt(0) - f[0], f[0])
        for q, (cx, cy, cz) in enumerate(VEL):
            if q == 0 or not 0 <= p - cx <= 1:
                continue
            e = near[p - cx, cy + 1, cz + 1, :, ys]
            g[q], moved = arrive(e, src[p, q, :, ys], f[OPP[q]], rebuilt(q), m)
            dm = dm + moved
        cx = 1 if p == 1 else -1
        total, jx, jy, jz, pxx, pyy, pzz, pxy, pxz = side_moments(cx, [g[q] for q in side_dirs(cx)])
        pp, mm, pm, mp = (g[INDEX[(0, b, c)]] for b, c in ((1, 1), (-1, -1), (1, -1), (-1, 1)))
        diag, anti = pp + mm, pm + mp
        yy, zz = g[3] + g[4], g[5] + g[6]
        rho = total + g[0] + yy + zz + (diag + anti)
        jy = jy + (g[3] - g[4]) + (pp - mm) + (pm - mp)
        jz = jz + (g[5] - g[6]) + (pp - mm) - (pm - mp)
        pyy = pyy + yy + (diag + anti)
        pzz = pzz + zz + (diag + anti)
        pyz = diag - anti
        for k, value in enumerate((rho, jx, jy, jz, pxx, pyy, pzz, pxy, pxz, pyz, dm, lift, *j0)):
            part[p, k, :, ys] = value

    def finish(t, p, h):
        ys = half(h)
        cx = 1 if p == 0 else -1
        kind, m = flags[t, p, :, ys], mass[t, p, :, ys]
        rho, jx, jy, jz, pxx, pyy, pzz, pxy, pxz, pyz, dm, lift, ax, ay, az = (part[p, k, :, ys] for k in range(15))
        sources = far_sources(t, p, h)
        g = []
        for k, q in enumerate(side_dirs(cx)):
            cy, cz = OFFS[k]
            proj = ax if cx == 1 else -ax
            if cy:
                proj = proj + (ay if cy == 1 else -ay)
            if cz:
                proj = proj + (az if cz == 1 else -az)
            rebuilt = WEIGHT[q] * (lift + 9.0 * (proj * proj))
            value, moved = arrive(far[p, k, :, ys], sources[k], pops[t, OPP[q], p, :, ys], rebuilt, m)
            g.append(value)
            dm = dm + moved
        more = side_moments(cx, g)
        rho, jx, jy, jz, pxx, pyy, pzz, pxy, pxz = (
            a + b for a, b in zip((rho, jx, jy, jz, pxx, pyy, pzz, pxy, pxz), more)
        )
        is_face, is_liquid = kind == 1, kind == 2
        mass_new = jnp.where(is_face, m + dm, jnp.where(is_liquid, rho, 0.0))
        fluid = is_face | is_liquid
        third = rho * (1.0 / 3.0)
        xx, yy, zz = jx * jx, jy * jy, jz * jz
        strength = (1.0 - relax[p, :, ys]) * 4.5
        qxx, qyy, qzz = pxx - third - xx, pyy - third - yy, pzz - third - zz
        mean = (qxx + qyy + qzz) * (1.0 / 3.0)
        qxx, qyy, qzz, mean = strength * qxx, strength * qyy, strength * qzz, strength * mean
        four = 4.0 * strength
        qxy, qxz, qyz = four * (pxy - jx * jy), four * (pxz - jx * jz), four * (pyz - jy * jz)
        base = rho - 1.5 * (xx + yy + zz) - mean
        new = {0: W0 * base}

        def couple(q, proj, stress):
            w = WEIGHT[q]
            even = w * (base + 4.5 * (proj * proj) + stress)
            odd = (3.0 * w) * proj
            new[q], new[OPP[q]] = even + odd, even - odd

        couple(1, jx, qxx)
        couple(3, jy, qyy)
        couple(5, jz, qzz)
        couple(INDEX[(1, 1, 0)], jx + jy, qxx + qyy + qxy)
        couple(INDEX[(1, -1, 0)], jx - jy, qxx + qyy - qxy)
        couple(INDEX[(1, 0, 1)], jx + jz, qxx + qzz + qxz)
        couple(INDEX[(1, 0, -1)], jx - jz, qxx + qzz - qxz)
        couple(INDEX[(0, 1, 1)], jy + jz, qyy + qzz + qyz)
        couple(INDEX[(0, 1, -1)], jy - jz, qyy + qzz - qyz)
        new = [jnp.where(fluid, new[q], WEIGHT[q]) for q in range(19)]
        if t == 1:
            mass_out[p, :, ys] = mass_new
            for q in range(19):
                pops_out[q, p, :, ys] = new[q]
            return
        for k, q in enumerate(side_dirs(2 * p - 1)):
            sx[1, p, h, k] = new[q]
        code_new = code_of(flags[1, p, :, ys], mass_new)
        sc[1, p, :, ys] = code_new
        code[1, p, :, ys] = code_new
        mass[1, p, :, ys] = mass_new
        for q in range(19):
            pops[1, q, p, :, ys] = new[q]

    for t in (0, 1):
        for u in (0, 1):
            send_y(t, u).wait_recv()
        stream(t)
        for d in (0, 1):
            send_code(t, 1 - d).wait_recv()
            for u in (0, 1):
                send_corner(t, 1 - d, u).wait_recv()
            far_codes(t, d)
        for p in (0, 1):
            for h in (0, 1):
                interior(t, p, h)
        for p in (0, 1):
            if t == 1:
                for h in (0, 1):
                    send_pops(t, 1 - p, h).wait_recv()
            for h in (0, 1):
                if t == 0:
                    send_pops(t, 1 - p, h).wait_recv()
                finish(t, p, h)
                if t == 0:
                    if h == 1:
                        send_code(1, p).start()
                    send_pops(1, p, h).start()
            if t == 0:
                fill_corner(1, p)
                for u in (0, 1):
                    send_corner(1, p, u).start()
        if t == 0:
            fill_y(1)
            for u in (0, 1):
                send_y(1, u).start()

    for t in (0, 1):
        for d in (0, 1):
            send_code(t, d).wait_send()
            for h in (0, 1):
                send_pops(t, d, h).wait_send()
                send_corner(t, d, h).wait_send()
            send_y(t, d).wait_send()


def on_device(populations, mass, flags, relax):
    _, planes, depth, width = populations.shape
    tile, plane = (depth, LANES), (depth, width)
    f32 = jnp.float32
    vmem, dma = pltpu.VMEM, pltpu.SemaphoreType.DMA
    hbm = pl.BlockSpec(memory_space=pltpu.HBM)
    here = pl.BlockSpec(memory_space=pltpu.VMEM)
    return pl.pallas_call(
        kernel,
        out_shape=(
            jax.ShapeDtypeStruct(populations.shape, f32),
            jax.ShapeDtypeStruct(mass.shape, f32),
        ),
        in_specs=[hbm] * 4,
        out_specs=(here, here),
        scratch_shapes=[
            vmem((2, 19, planes, *plane), f32),
            vmem((2, planes, *plane), f32),
            vmem((2, planes, *plane), jnp.int32),
            vmem((planes, *plane), f32),
            vmem((2, planes, *plane), f32),
            vmem((planes, 19, *plane), f32),
            vmem((planes, 3, 3, *plane), f32),
            vmem((2, 5, *plane), f32),
            vmem((planes, 15, *plane), f32),
            vmem((2, 2, 2, 5, *tile), f32),
            vmem((2, 2, 2, 5, *tile), f32),
            vmem((2, 2, *plane), f32),
            vmem((2, 2, *plane), f32),
            vmem((2, 2, *tile), f32),
            vmem((2, 2, *tile), f32),
            vmem((2, 2, 2, *tile), f32),
            vmem((2, 2, 2, *tile), f32),
            dma((4,)),
            dma((2, 2, 2)),
            dma((2, 2, 2)),
            dma((2, 2)),
            dma((2, 2)),
            dma((2, 2)),
            dma((2, 2)),
            dma((2, 2, 2)),
            dma((2, 2, 2)),
        ],
        compiler_params=pltpu.CompilerParams(
            collective_id=0, has_side_effects=True, vmem_limit_bytes=32 * 1024 * 1024
        ),
        name="lattice_steps",
    )(populations, mass, flags, relax)


def solution(mesh):
    return jax.shard_map(
        on_device,
        mesh=mesh,
        in_specs=(
            P(None, "gx", None, "gy"),
            P("gx", None, "gy"),
            P(None, "gx", None, "gy"),
            P("gx", None, "gy"),
        ),
        out_specs=(P(None, "gx", None, "gy"), P("gx", None, "gy")),
        check_vma=False,
    )
```

time: 172 us -> 45 us (0.26); the launches traced: 169 us -> 44.7 us
  local copies, waits for them, and re-layouts: 54.5 us -> 4.87 us
  starting transfers between devices: 43.4 us -> 0 us
  Pallas kernels: 0 us -> 39.2 us
  waiting for transfers between devices: 38.2 us -> 0 us
  other arithmetic: 20 us -> 0 us
  matrix products: 11.7 us -> 0 us
    ppermute x8 -> x0, starting transfers between devices: 43.4 us -> none  [the longest x4 25.3 us: padded_2(): lax.ppermute(head, axis, [((i + 1) % count, i) for i in range(count)])]
    pallas_call x0 -> x1, Pallas kernels: none -> 39.2 us  [on_device(): pl.pallas_call(kernel, out_shape=(jax.ShapeDtypeStruct(populations.shape,...]
    ppermute x8 -> x0, waiting for transfers between devices: 38.2 us -> none  [the longest x4 28.2 us: padded_2(): lax.ppermute(tail, axis, [(i, (i + 1) % count) for i in range(count)])]
    slice x30 -> x0, local copies, waits for them, and re-layouts: 27.2 us -> none  [the longest x20 17.8 us: advance(): reverse = jnp.stack([pops[other] for other in opposite_index])]
    another operation x6 -> x0, local copies, waits for them, and re-layouts: 20.6 us -> none  [the longest x2 6.97 us: advance(): source_pop = jnp.stack(source_pop)]
    dot_general x12 -> x0, matrix products: 11.7 us -> none  [the longest x2 3.32 us: advance(): momentum_old = jnp.tensordot(velocity.T, pops, axes=1, precision=highest)]
    concatenate x10 -> x0, other arithmetic: 8.71 us -> none  [the longest x8 8.55 us: padded_2(): jnp.concatenate([lax.ppermute(tail, axis, [(i, (i + 1) % count) for i in...]
    reduce_sum x4 -> x0, other arithmetic: 4.73 us -> none  [the longest x2 3.18 us: advance(): moved_mass = jnp.sum((share * (source_pop - reverse))[1:], 0)]
  transfers between devices with their start and end apart: 8 -> 0, of which waited for: 5 -> 0; matrix products, arithmetic and copies ran while one was open for 14% -> 0% of each run, Pallas kernels for 0% -> 0%
where the time goes in v1:
time: 45 us; the launch traced here: 44.7 us
  Pallas kernels  39.2 us (87%)
  local copies, waits for them, and re-layouts  4.87 us (11%)
  between operations  0.65 us (1%)
    pallas_call x1, Pallas kernels, on_device(): pl.pallas_call(kernel, out_shape=(jax.ShapeDtypeStruct(populations.shape,...  39.2 us
    unnamed x10, local copies, waits for them, and re-layouts  4.87 us

profile of v1, /device:TPU:1, one launch (start us, length us, event | category | flops | bytes accessed | tf_op | source)
XLA Modules:
  0.0 44.7 jit_solution(16594173341459047678)
XLA Ops:
  0.6 0.0 copy-start
  0.6 1.1 %copy-done = f32[19,2,16,256]{3,2,1,0:T(8,128)S(1)} copy-done((f32[19,2,16,256]{3,2,1,0:T(8,128)S(1)}, f32[19,2,16,256]{3,2,1,0:T(8,128)}, u32[]{:S(2)}) %copy-start) | copy-done | bytes 622616
  1.7 0.0 copy-start.1
  1.7 0.8 %copy-done.1 = s32[2,2,16,256]{3,2,1,0:T(8,128)S(1)} copy-done((s32[2,2,16,256]{3,2,1,0:T(8,128)S(1)}, s32[2,2,16,256]{3,2,1,0:T(8,128)}, u32[]{:S(2)}) %copy-start.1) | copy-done | bytes 65560
  2.5 0.0 copy-start.2
  2.5 0.8 %copy-done.2 = f32[2,16,256]{2,1,0:T(8,128)S(1)} copy-done((f32[2,16,256]{2,1,0:T(8,128)S(1)}, f32[2,16,256]{2,1,0:T(8,128)}, u32[]{:S(2)}) %copy-start.2) | copy-done | bytes 32792
  3.3 0.0 copy-start.3
  3.3 0.8 %copy-done.3 = f32[2,16,256]{2,1,0:T(8,128)S(1)} copy-done((f32[2,16,256]{2,1,0:T(8,128)S(1)}, f32[2,16,256]{2,1,0:T(8,128)}, u32[]{:S(2)}) %copy-start.3) | copy-done | bytes 32792
  4.1 39.2 %lattice_steps.1 = (f32[19,2,16,256]{3,2,1,0:T(8,128)S(1)}, f32[2,16,256]{2,1,0:T(8,128)S(1)}) custom-call(f32[19,2,16,256]{3,2,1,0:T(8,128)S(1)} %copy-done, f32[2,16,256]{2,1,0:T(8,128)S(1)} %copy-done.2, s32[2,2,16,256]{3,2,1,0:T(8,128)S(1)} %copy-done.1, f32[2,16,256]{2,1,0:T(8,128)S(1)} %copy-done.3), custom_call_target="tpu_custom_call" | custom-call | tf_op jit(solution)/shard_map/lattice_steps/pallas_call | solution.py:470
  43.2 0.8 %copy.8 = f32[19,2,16,256]{3,2,1,0:T(8,128)} copy(f32[19,2,16,256]{3,2,1,0:T(8,128)S(1)} %get-tuple-element.4) | data formatting | bytes 1245184
  44.1 0.6 %copy.9 = f32[2,16,256]{2,1,0:T(8,128)} copy(f32[2,16,256]{2,1,0:T(8,128)S(1)} %get-tuple-element.5) | data formatting | bytes 65536
Async XLA Ops:
  0.6 1.1 %copy-start = (f32[19,2,16,256]{3,2,1,0:T(8,128)S(1)}, f32[19,2,16,256]{3,2,1,0:T(8,128)}, u32[]{:S(2)}) copy-start(f32[19,2,16,256]{3,2,1,0:T(8,128)} %pops_in.1) | copy-start | bytes 1867780
  1.7 0.8 %copy-start.1 = (s32[2,2,16,256]{3,2,1,0:T(8,128)S(1)}, s32[2,2,16,256]{3,2,1,0:T(8,128)}, u32[]{:S(2)}) copy-start(s32[2,2,16,256]{3,2,1,0:T(8,128)} %flags_in.1) | copy-start | bytes 196612
  2.5 0.8 %copy-start.2 = (f32[2,16,256]{2,1,0:T(8,128)S(1)}, f32[2,16,256]{2,1,0:T(8,128)}, u32[]{:S(2)}) copy-start(f32[2,16,256]{2,1,0:T(8,128)} %mass_in.1) | copy-start | bytes 98308
  3.3 0.8 %copy-start.3 = (f32[2,16,256]{2,1,0:T(8,128)S(1)}, f32[2,16,256]{2,1,0:T(8,128)}, u32[]{:S(2)}) copy-start(f32[2,16,256]{2,1,0:T(8,128)} %relax_in.1) | copy-start | bytes 98308

commit v2 on v1

--- a/solution.py
+++ b/solution.py
@@ -139,6 +139,9 @@
     y_id = [(gx, down), (gx, up)]
     corner_id = [[(left, down), (left, up)], [(right, down), (right, up)]]
 
+    barrier = pltpu.get_barrier_semaphore()
+    for other in side_id + y_id + corner_id[0] + corner_id[1]:
+        pl.semaphore_signal(barrier, inc=1, device_id=other, device_id_type=MESH)
     loads = [
         pltpu.make_async_copy(mass_in, mass.at[0], load_sem.at[0]),
         pltpu.make_async_copy(flags_in, flags, load_sem.at[1]),
@@ -147,9 +150,6 @@
     ]
     for load in loads:
         load.start()
-    barrier = pltpu.get_barrier_semaphore()
-    for other in side_id + y_id + corner_id[0] + corner_id[1]:
-        pl.semaphore_signal(barrier, inc=1, device_id=other, device_id_type=MESH)
 
     def send_code(t, d):
         return pltpu.make_async_remote_copy(
@@ -460,19 +460,32 @@
             send_y(t, d).wait_send()
 
 
+def write_back(pops, mass, pops_out, mass_out, sem):
+    copies = [
+        pltpu.make_async_copy(pops, pops_out, sem.at[0]),
+        pltpu.make_async_copy(mass, mass_out, sem.at[1]),
+    ]
+    for copy in copies:
+        copy.start()
+    for copy in copies:
+        copy.wait()
+
+
 def on_device(populations, mass, flags, relax):
     _, planes, depth, width = populations.shape
     tile, plane = (depth, LANES), (depth, width)
     f32 = jnp.float32
     vmem, dma = pltpu.VMEM, pltpu.SemaphoreType.DMA
+    state_shape = (
+        jax.ShapeDtypeStruct(populations.shape, f32),
+        jax.ShapeDtypeStruct(mass.shape, f32),
+    )
     hbm = pl.BlockSpec(memory_space=pltpu.HBM)
     here = pl.BlockSpec(memory_space=pltpu.VMEM)
-    return pl.pallas_call(
+    args = [pltpu.with_memory_space_constraint(a, pltpu.HBM) for a in (populations, mass, flags, relax)]
+    state = pl.pallas_call(
         kernel,
-        out_shape=(
-            jax.ShapeDtypeStruct(populations.shape, f32),
-            jax.ShapeDtypeStruct(mass.shape, f32),
-        ),
+        out_shape=state_shape,
         in_specs=[hbm] * 4,
         out_specs=(here, here),
         scratch_shapes=[
@@ -507,7 +520,16 @@
             collective_id=0, has_side_effects=True, vmem_limit_bytes=32 * 1024 * 1024
         ),
         name="lattice_steps",
-    )(populations, mass, flags, relax)
+    )(*args)
+    anywhere = pl.BlockSpec(memory_space=pl.ANY)
+    return pl.pallas_call(
+        write_back,
+        out_shape=state_shape,
+        in_specs=[here] * 2,
+        out_specs=(anywhere,) * 2,
+        scratch_shapes=[dma((2,))],
+        name="write_back",
+    )(*(pltpu.with_memory_space_constraint(a, pltpu.VMEM) for a in state))
 
 
 def solution(mesh):

time: 45 us -> 40.5 us (0.900)
  local copies, waits for them, and re-layouts: 4.87 us -> 0 us
  Pallas kernels: 39.2 us -> 39.7 us
    unnamed x10 -> x0, local copies, waits for them, and re-layouts: 4.87 us -> none
    pallas_call x1 -> x2, Pallas kernels: 39.2 us -> 39.7 us  [the longest x1 38.8 us: on_device(): pl.pallas_call(kernel, out_shape=state_shape, in_specs=[hbm] * 4, out_spe...]
where the time goes in v2:
time: 40.5 us; the launch traced here: 40.3 us
  Pallas kernels  39.7 us (98%)
  between operations  0.64 us (2%)
    pallas_call x1, Pallas kernels, on_device(): pl.pallas_call(kernel, out_shape=state_shape, in_specs=[hbm] * 4, out_spe...  38.8 us
    pallas_call x1, Pallas kernels, on_device(): pl.pallas_call(write_back, out_shape=state_shape, in_specs=[here] * 2, ou...  0.85 us

profile of v2, /device:TPU:1, one launch (start us, length us, event | category | flops | bytes accessed | tf_op | source)
XLA Modules:
  0.0 40.3 jit_solution(6273830990725906539)
XLA Ops:
  0.6 38.8 %lattice_steps.1 = (f32[19,2,16,256]{3,2,1,0:T(8,128)S(1)}, f32[2,16,256]{2,1,0:T(8,128)S(1)}) custom-call(f32[19,2,16,256]{3,2,1,0:T(8,128)} %pops_in.1, f32[2,16,256]{2,1,0:T(8,128)} %mass_in.1, s32[2,2,16,256]{3,2,1,0:T(8,128)} %flags_in.1, f32[2,16,256]{2,1,0:T(8,128)} %relax_in.1), custom_call_target="tpu_custom_call" | custom-call | tf_op jit(solution)/shard_map/lattice_steps/pallas_call | solution.py:486
  39.5 0.8 %write_back.1 = (f32[19,2,16,256]{3,2,1,0:T(8,128)}, f32[2,16,256]{2,1,0:T(8,128)}) custom-call(f32[19,2,16,256]{3,2,1,0:T(8,128)S(1)} %get-tuple-element.4.pops, f32[2,16,256]{2,1,0:T(8,128)S(1)} %get-tuple-element.5.mass), custom_call_target="tpu_custom_call" | custom-call | tf_op jit(solution)/shard_map/write_back/pallas_call | solution.py:525

commit v3 on v2

v3 whole, which is shorter than its diff:
```python
import jax
import jax.numpy as jnp
from jax import lax
from jax.experimental import pallas as pl
from jax.experimental.pallas import tpu as pltpu
from jax.sharding import PartitionSpec as P

MESH = pl.DeviceIdType.MESH

VEL = [
    (0, 0, 0),
    (1, 0, 0),
    (-1, 0, 0),
    (0, 1, 0),
    (0, -1, 0),
    (0, 0, 1),
    (0, 0, -1),
    (1, 1, 0),
    (-1, -1, 0),
    (1, -1, 0),
    (-1, 1, 0),
    (1, 0, 1),
    (-1, 0, -1),
    (1, 0, -1),
    (-1, 0, 1),
    (0, 1, 1),
    (0, -1, -1),
    (0, 1, -1),
    (0, -1, 1),
]
INDEX = {c: q for q, c in enumerate(VEL)}
OPP = [INDEX[(-a, -b, -c)] for a, b, c in VEL]
W0, W1, W2 = 1.0 / 3.0, 1.0 / 18.0, 1.0 / 36.0
WEIGHT = [W0] + [W1] * 6 + [W2] * 12
SIGMA = 0.02
OFFS = [(0, 0), (1, 0), (-1, 0), (0, 1), (0, -1)]
IN_PLANE = [(1, 0), (-1, 0), (0, 1), (0, -1), (1, 1), (-1, -1), (1, -1), (-1, 1)]
LANES = 128
ROWS = 8


OPP_OFFS = [0, 2, 1, 4, 3]
CHUNKS = [(zh, h) for h in (0, 1) for zh in (0, 1)]


def side_dirs(cx):
    return [INDEX[(cx, b, c)] for b, c in OFFS]


def y_columns(cy):
    cols = []
    for plane in (0, 1):
        for cz in (0, 1, -1):
            cols.append((INDEX[(0, cy, cz)], plane))
        cols.append((INDEX[(1 - 2 * plane, cy, 0)], plane))
        cols.append((None, plane))
    return cols


def frac_of(e):
    return jnp.where(e == 1.0, 1.0, jnp.where(e > 1.5, e - 2.0, 0.0))


def code_of(kind, mass):
    return jnp.where(kind == 3, -1.0, jnp.where(kind == 0, 0.0, jnp.where(kind == 2, 1.0, 2.0 + mass)))


def half(h):
    return slice(h * LANES, (h + 1) * LANES)


def shift_y(halves, cy, column):
    lane = lax.broadcasted_iota(jnp.int32, halves[0].shape, 1)
    if cy == 1:
        moved = [pltpu.roll(a, 1, 1) for a in halves]
        edge = lane == 0
        return [jnp.where(edge, column, moved[0]), jnp.where(edge, moved[0], moved[1])]
    moved = [pltpu.roll(a, LANES - 1, 1) for a in halves]
    edge = lane == LANES - 1
    return [jnp.where(edge, moved[1], moved[0]), jnp.where(edge, column, moved[1])]


def shift_z(halves, cz):
    depth = halves[0].shape[0]
    return [pltpu.roll(a, cz % depth, 0) for a in halves]


def wall_z(halves, cz):
    row = lax.broadcasted_iota(jnp.int32, halves[0].shape, 0)
    outside = row == (0 if cz == 1 else halves[0].shape[0] - 1)
    return [jnp.where(outside, -1.0, a) for a in shift_z(halves, cz)]


def rows(z):
    return slice(z * ROWS, (z + 1) * ROWS)


def spread(tile, k):
    low, high = tile[:, 2 * k : 2 * k + 1], tile[:, 2 * k + 1 : 2 * k + 2]
    return jnp.concatenate([jnp.broadcast_to(low, tile.shape), jnp.broadcast_to(high, tile.shape)], axis=0)


def pack(columns):
    lane = lax.broadcasted_iota(jnp.int32, (ROWS, LANES), 1)
    tile = jnp.zeros(lane.shape, jnp.float32)
    for k, column in enumerate(columns):
        for z in (0, 1):
            tile = jnp.where(lane == 2 * k + z, jnp.broadcast_to(column[rows(z)], lane.shape), tile)
    return tile


def kernel(
    pops_in,
    mass_in,
    flags_in,
    relax_in,
    pops_out,
    mass_out,
    pops,
    mass,
    flags,
    relax,
    code,
    inner,
    cross,
    near,
    far,
    part,
    sx,
    rx,
    sc,
    rc,
    sy,
    ry,
    sk,
    rk,
    load_sem,
    sx_sem,
    rx_sem,
    sc_sem,
    rc_sem,
    sy_sem,
    ry_sem,
    sk_sem,
    rk_sem,
):
    nx, ny = lax.axis_size("gx"), lax.axis_size("gy")
    gx, gy = lax.axis_index("gx"), lax.axis_index("gy")
    ys = [lax.rem(gy + ny - 1, ny), gy, lax.rem(gy + 1, ny)]
    sides = [lax.rem(gx, 2), lax.rem(gx + 1, 2)]

    def device(d, u):
        return (lax.rem(gx + 2 * d - 1 + nx, nx), ys[u + 1])

    barrier = pltpu.get_barrier_semaphore()
    for d in sides:
        for u in (0, -1, 1):
            pl.semaphore_signal(barrier, inc=1, device_id=device(d, u), device_id_type=MESH)
    for u in (-1, 1):
        pl.semaphore_signal(barrier, inc=1, device_id=(gx, ys[u + 1]), device_id_type=MESH)
    loads = [
        pltpu.make_async_copy(mass_in, mass.at[0], load_sem.at[0]),
        pltpu.make_async_copy(flags_in, flags, load_sem.at[1]),
        pltpu.make_async_copy(pops_in, pops.at[0], load_sem.at[2]),
        pltpu.make_async_copy(relax_in, relax, load_sem.at[3]),
    ]
    for load in loads:
        load.start()

    def x_code(d, at):
        return pltpu.make_async_remote_copy(
            sc.at[d], rc.at[at], sc_sem.at[d], rc_sem.at[at], device_id=device(d, 0), device_id_type=MESH
        )

    def x_chunk(t, d, c, at):
        count = pl.ds(0, 5 + t)
        return pltpu.make_async_remote_copy(
            sx.at[t, d, c, count],
            rx.at[t, at, c, count],
            sx_sem.at[t, d, c],
            rx_sem.at[t, at, c],
            device_id=device(d, 0),
            device_id_type=MESH,
        )

    def x_corner(t, d, u, at):
        return pltpu.make_async_remote_copy(
            sk.at[t, d, u],
            rk.at[t, at[0], at[1]],
            sk_sem.at[t, d, u],
            rk_sem.at[t, at[0], at[1]],
            device_id=device(d, 2 * u - 1),
            device_id_type=MESH,
        )

    def y_tile(t, u, at):
        return pltpu.make_async_remote_copy(
            sy.at[t, u], ry.at[t, at], sy_sem.at[t, u], ry_sem.at[t, at], device_id=(gx, ys[2 * u]), device_id_type=MESH
        )

    def pick(pair, p):
        return pair[0] + p * (pair[1] - pair[0])

    plus, minus = side_dirs(1), side_dirs(-1)
    inward = list(zip(plus, minus))
    outward = list(zip(minus, plus))

    def rim_of(t, q, p, u):
        at = 0 if u == 0 else 2 * LANES - 1
        if q is None:
            return code[t, p, :, at : at + 1]
        return pops[t, q, p, :, at : at + 1]

    def fill_y(t):
        for u in (0, 1):
            sy[t, u] = pack([rim_of(t, q, p, u) for q, p in y_columns(2 * u - 1)])

    def fill_corner(t, p):
        for u in (0, 1):
            q = pick(outward[2 - u], p)
            sk[t, p, u] = pack([rim_of(t, q, p, u), rim_of(t, None, p, u)])

    loads[0].wait()
    loads[1].wait()
    for p in (0, 1):
        code[0, p] = code_of(flags[0, p], mass[0, p])
        sc[p] = code[0, p]
    loads[2].wait()
    for p in (0, 1):
        fill_corner(0, p)
        for k, (cy, cz) in enumerate(OFFS):
            halves = [pops[0, outward[k][p], p, :, half(h)] for h in (0, 1)]
            if cy:
                halves = shift_y(halves, cy, halves[0])
            if cz:
                halves = shift_z(halves, cz)
            for c, (z, h) in enumerate(CHUNKS):
                sx[0, p, c, k] = halves[h][rows(z)]
    fill_y(0)
    loads[3].wait()

    pl.semaphore_wait(barrier, 8)
    for i, d in enumerate(sides):
        for u in (0, 1):
            x_corner(0, d, u, (1 - d, 1 - u)).start()
        x_code(d, 1 - d).start()
        for c in range(4):
            x_chunk(0, d, c, 1 - d).start()
        if i == 0:
            for u in (0, 1):
                y_tile(0, u, 1 - u).start()

    def stream(t):
        place = [{c: k for k, c in enumerate(y_columns(cy))} for cy in (1, -1)]

        def column(q, p, cy):
            u = 0 if cy == 1 else 1
            return spread(ry[t, u], place[u][(q, p)])

        def moved(q, p, cy, cz):
            halves = [pops[t, q, p, :, half(h)] for h in (0, 1)]
            if cy:
                halves = shift_y(halves, cy, column(q, p, cy))
            if cz:
                halves = shift_z(halves, cz)
            return halves

        for p in (0, 1):
            own = [code[t, p, :, half(h)] for h in (0, 1)]
            table = {(0, 0): own}
            for cy in (1, -1):
                table[(cy, 0)] = shift_y(own, cy, column(None, p, cy))
            for cy in (0, 1, -1):
                for cz in (1, -1):
                    table[(cy, cz)] = wall_z(table[(cy, 0)], cz)
            for (cy, cz), halves in table.items():
                for h in (0, 1):
                    near[p, cy + 1, cz + 1, :, half(h)] = halves[h]
            for k, (cy, cz) in enumerate(IN_PLANE):
                halves = moved(INDEX[(0, cy, cz)], p, cy, cz)
                for h in (0, 1):
                    inner[p, k, :, half(h)] = halves[h]
            for k, (cy, cz) in enumerate(OFFS):
                halves = moved(outward[k][p], 1 - p, cy, cz)
                for h in (0, 1):
                    cross[p, k, :, half(h)] = halves[h]

    def plane_code(t, p):
        if t == 0:
            return [rc[p, :, half(h)] for h in (0, 1)]
        return [jnp.concatenate([rx[1, p, 2 * h, 5], rx[1, p, 2 * h + 1, 5]], axis=0) for h in (0, 1)]

    def far_codes(t, p):
        own = plane_code(t, p)
        for k, (cy, cz) in enumerate(OFFS):
            halves = own
            if cy:
                halves = shift_y(own, cy, spread(rk[t, p, 0 if cy == 1 else 1], 1))
            if cz:
                halves = wall_z(own, cz)
            for h in (0, 1):
                far[p, k, :, half(h)] = halves[h]

    def arrive(e, s, r, rebuilt, m):
        g = jnp.where(e == -1.0, r, jnp.where(e == 0.0, rebuilt - r, s))
        a = jnp.where(e == 1.0, 1.0, jnp.where(e > 1.5, 0.5 * (m + (e - 2.0)), 0.0))
        return g, a * (s - r)

    def side_moments(g):
        total = (g[0] + g[1]) + (g[2] + (g[3] + g[4]))
        return [total, g[1] - g[2], g[3] - g[4], g[1] + g[2], g[3] + g[4]]

    def interior(t, p, h, x_far):
        lanes = half(h)
        kind, m = flags[t, p, :, lanes], mass[t, p, :, lanes]
        rest = pops[t, 0, p, :, lanes]
        flat = [pops[t, INDEX[(0, cy, cz)], p, :, lanes] for cy, cz in IN_PLANE]
        fin = [pops[t, pick(inward[k], p), p, :, lanes] for k in range(5)]
        fout = [pops[t, pick(outward[k], p), p, :, lanes] for k in range(5)]
        tin, yin, zin, _, _ = side_moments(fin)
        tout, yout, zout, _, _ = side_moments(fout)
        pp, mm, pm, mp = flat[4:]
        ax = tin - tout
        ay = (yin + yout) + (flat[0] - flat[1]) + (pp - mm) + (pm - mp)
        az = (zin + zout) + (flat[2] - flat[3]) + (pp - mm) - (pm - mp)
        own = jnp.where(kind == 2, 1.0, jnp.where(kind == 1, m, 0.0))
        around = frac_of(x_far) + frac_of(near[1 - p, 1, 1, :, lanes])
        for cy, cz in OFFS[1:]:
            around = around + frac_of(near[p, cy + 1, cz + 1, :, lanes])
        gas = 1.0 - 3.0 * SIGMA * (around - 6.0 * own)
        lift = 2.0 * gas - 3.0 * (ax * ax + ay * ay + az * az)

        dm = jnp.zeros_like(m)
        e0 = near[p, 1, 1, :, lanes]
        g0 = jnp.where(e0 == 0.0, W0 * lift - rest, rest)
        g = []
        for k, (cy, cz) in enumerate(IN_PLANE):
            proj = sum(c * j for c, j in ((cy, ay), (cz, az)) if c)
            w = W2 if cy and cz else W1
            value, moved = arrive(
                near[p, cy + 1, cz + 1, :, lanes],
                inner[p, k, :, lanes],
                flat[k ^ 1],
                w * (lift + 9.0 * (proj * proj)),
                m,
            )
            g.append(value)
            dm = dm + moved
        out = []
        for k, (cy, cz) in enumerate(OFFS):
            proj = -ax + sum(c * j for c, j in ((cy, ay), (cz, az)) if c)
            w = W2 if cy or cz else W1
            value, moved = arrive(
                near[1 - p, cy + 1, cz + 1, :, lanes],
                cross[p, k, :, lanes],
                fin[OPP_OFFS[k]],
                w * (lift + 9.0 * (proj * proj)),
                m,
            )
            out.append(value)
            dm = dm + moved
        total, dy, dz, yy2, zz2 = side_moments(out)
        pp, mm, pm, mp = g[4:]
        diag, anti = pp + mm, pm + mp
        yy, zz = g[0] + g[1], g[2] + g[3]
        rho = total + g0 + yy + zz + (diag + anti)
        jy = dy + (g[0] - g[1]) + (pp - mm) + (pm - mp)
        jz = dz + (g[2] - g[3]) + (pp - mm) - (pm - mp)
        pyy = yy2 + yy + (diag + anti)
        pzz = zz2 + zz + (diag + anti)
        kept = (rho, total, jy, jz, pyy, pzz, dy, dz, diag - anti, dm, lift, ax, ay, az)
        for k, value in enumerate(kept):
            part[p, k, :, lanes] = value

    def finish(t, p, z, lanes, sources):
        kind, m = flags[t, p, z, lanes], mass[t, p, z, lanes]
        rho, tout, jy, jz, pyy, pzz, dyout, dzout, pyz, dm, lift, ax, ay, az = (
            part[p, k, z, lanes] for k in range(14)
        )
        g = []
        for k, (cy, cz) in enumerate(OFFS):
            proj = ax + sum(c * j for c, j in ((cy, ay), (cz, az)) if c)
            w = W2 if cy or cz else W1
            value, moved = arrive(
                far[p, k, z, lanes],
                sources[k],
                pops[t, pick(outward[OPP_OFFS[k]], p), p, z, lanes],
                w * (lift + 9.0 * (proj * proj)),
                m,
            )
            g.append(value)
            dm = dm + moved
        total, dy, dz, yy2, zz2 = side_moments(g)
        rho, jx, pxx = rho + total, total - tout, total + tout
        jy, jz, pyy, pzz = jy + dy, jz + dz, pyy + yy2, pzz + zz2
        pxy, pxz = dy - dyout, dz - dzout
        is_face, is_liquid = kind == 1, kind == 2
        mass_new = jnp.where(is_face, m + dm, jnp.where(is_liquid, rho, 0.0))
        fluid = is_face | is_liquid
        third = rho * (1.0 / 3.0)
        xx, yy, zz = jx * jx, jy * jy, jz * jz
        strength = (1.0 - relax[p, z, lanes]) * 4.5
        qxx, qyy, qzz = pxx - third - xx, pyy - third - yy, pzz - third - zz
        mean = (qxx + qyy + qzz) * (1.0 / 3.0)
        qxx, qyy, qzz, mean = strength * qxx, strength * qyy, strength * qzz, strength * mean
        four = 4.0 * strength
        qxy, qxz, qyz = four * (pxy - jx * jy), four * (pxz - jx * jz), four * (pyz - jy * jz)
        base = rho - 1.5 * (xx + yy + zz) - mean

        def couple(w, proj, stress):
            even = w * (base + 4.5 * (proj * proj) + stress)
            odd = (3.0 * w) * proj
            return jnp.where(fluid, even + odd, w), jnp.where(fluid, even - odd, w)

        new_in, new_out = [None] * 5, [None] * 5
        new_in[0], new_out[0] = couple(W1, jx, qxx)
        new_in[1], new_out[2] = couple(W2, jx + jy, qxx + qyy + qxy)
        new_in[2], new_out[1] = couple(W2, jx - jy, qxx + qyy - qxy)
        new_in[3], new_out[4] = couple(W2, jx + jz, qxx + qzz + qxz)
        new_in[4], new_out[3] = couple(W2, jx - jz, qxx + qzz - qxz)
        flat = [
            *couple(W1, jy, qyy),
            *couple(W1, jz, qzz),
            *couple(W2, jy + jz, qyy + qzz + qyz),
            *couple(W2, jy - jz, qyy + qzz - qyz),
        ]
        new = [(0, jnp.where(fluid, W0 * base, W0))]
        new += [(INDEX[(0, cy, cz)], flat[k]) for k, (cy, cz) in enumerate(IN_PLANE)]
        new += [(pick(inward[k], p), new_in[k]) for k in range(5)]
        new += [(pick(outward[k], p), new_out[k]) for k in range(5)]
        return mass_new, new, new_out

    def close(t, p):
        for u in (0, 1):
            x_corner(t, p, u, (p, u)).wait_recv()
        if t == 0:
            x_code(p, p).wait_recv()
            far_codes(0, p)
            for h in (0, 1):
                interior(0, p, h, far[p, 0, :, half(h)])
            for c, (z, h) in enumerate(CHUNKS):
                x_chunk(0, p, c, p).wait_recv()
                sources = [rx[0, p, c, k] for k in range(5)]
                lane = lax.broadcasted_iota(jnp.int32, sources[0].shape, 1)
                k, edge, u = (1, lane == 0, 0) if h == 0 else (2, lane == LANES - 1, 1)
                column = jnp.broadcast_to(rk[0, p, u][:, z : z + 1], lane.shape)
                sources[k] = jnp.where(edge, column, sources[k])
                z, lanes = rows(z), half(h)
                mass_new, new, new_out = finish(0, p, z, lanes, sources)
                code_new = code_of(flags[1, p, z, lanes], mass_new)
                for k in range(5):
                    sx[1, p, c, k] = new_out[k]
                sx[1, p, c, 5] = code_new
                x_chunk(1, p, c, 1 - p).start()
                code[1, p, z, lanes] = code_new
                mass[1, p, z, lanes] = mass_new
                for q, value in new:
                    pops[1, q, p, z, lanes] = value
            fill_corner(1, p)
            for u in (0, 1):
                x_corner(1, p, u, (1 - p, 1 - u)).start()
            return
        for h in (0, 1):
            for z in (0, 1):
                x_chunk(1, p, 2 * h + z, p).wait_recv()
            interior(1, p, h, jnp.concatenate([rx[1, p, 2 * h, 5], rx[1, p, 2 * h + 1, 5]], axis=0))
        far_codes(1, p)
        beyond = []
        for k, (cy, cz) in enumerate(OFFS):
            halves = [jnp.concatenate([rx[1, p, 2 * h, k], rx[1, p, 2 * h + 1, k]], axis=0) for h in (0, 1)]
            if cy:
                halves = shift_y(halves, cy, spread(rk[1, p, 0 if cy == 1 else 1], 0))
            if cz:
                halves = shift_z(halves, cz)
            beyond.append(halves)
        for h in (0, 1):
            lanes = half(h)
            mass_new, new, _ = finish(1, p, slice(None), lanes, [halves[h] for halves in beyond])
            mass_out[p, :, lanes] = mass_new
            for q, value in new:
                pops_out[q, p, :, lanes] = value

    for t in (0, 1):
        for u in (0, 1):
            y_tile(t, u, u).wait_recv()
        stream(t)

        @pl.loop(0, 2)
        def _(i, t=t):
            close(t, lax.rem(gx + 1 + i, 2))

        if t == 0:
            fill_y(1)
            for u in (0, 1):
                y_tile(1, u, 1 - u).start()

    for d in (0, 1):
        x_code(d, 1 - d).wait_send()
        for t in (0, 1):
            for c in range(4):
                x_chunk(t, d, c, 1 - d).wait_send()
            for u in (0, 1):
                x_corner(t, d, u, (1 - d, 1 - u)).wait_send()
            y_tile(t, d, 1 - d).wait_send()


def write_back(pops, mass, pops_out, mass_out, sem):
    copies = [
        pltpu.make_async_copy(pops, pops_out, sem.at[0]),
        pltpu.make_async_copy(mass, mass_out, sem.at[1]),
    ]
    for copy in copies:
        copy.start()
    for copy in copies:
        copy.wait()


def on_device(populations, mass, flags, relax):
    _, planes, depth, width = populations.shape
    tile, plane = (ROWS, LANES), (depth, width)
    f32 = jnp.float32
    vmem, dma = pltpu.VMEM, pltpu.SemaphoreType.DMA
    state_shape = (
        jax.ShapeDtypeStruct(populations.shape, f32),
        jax.ShapeDtypeStruct(mass.shape, f32),
    )
    hbm = pl.BlockSpec(memory_space=pltpu.HBM)
    here = pl.BlockSpec(memory_space=pltpu.VMEM)
    args = [pltpu.with_memory_space_constraint(a, pltpu.HBM) for a in (populations, mass, flags, relax)]
    state = pl.pallas_call(
        kernel,
        out_shape=state_shape,
        in_specs=[hbm] * 4,
        out_specs=(here, here),
        scratch_shapes=[
            vmem((2, 19, planes, *plane), f32),
            vmem((2, planes, *plane), f32),
            vmem((2, planes, *plane), jnp.int32),
            vmem((planes, *plane), f32),
            vmem((2, planes, *plane), f32),
            vmem((planes, 8, *plane), f32),
            vmem((planes, 5, *plane), f32),
            vmem((planes, 3, 3, *plane), f32),
            vmem((2, 5, *plane), f32),
            vmem((planes, 14, *plane), f32),
            vmem((2, 2, 4, 6, *tile), f32),
            vmem((2, 2, 4, 6, *tile), f32),
            vmem((2, *plane), f32),
            vmem((2, *plane), f32),
            vmem((2, 2, *tile), f32),
            vmem((2, 2, *tile), f32),
            vmem((2, 2, 2, *tile), f32),
            vmem((2, 2, 2, *tile), f32),
            dma((4,)),
            dma((2, 2, 4)),
            dma((2, 2, 4)),
            dma((2,)),
            dma((2,)),
            dma((2, 2)),
            dma((2, 2)),
            dma((2, 2, 2)),
            dma((2, 2, 2)),
        ],
        compiler_params=pltpu.CompilerParams(
            collective_id=0, has_side_effects=True, vmem_limit_bytes=32 * 1024 * 1024
        ),
        name="lattice_steps",
    )(*args)
    anywhere = pl.BlockSpec(memory_space=pl.ANY)
    return pl.pallas_call(
        write_back,
        out_shape=state_shape,
        in_specs=[here] * 2,
        out_specs=(anywhere,) * 2,
        scratch_shapes=[dma((2,))],
        name="write_back",
    )(*(pltpu.with_memory_space_constraint(a, pltpu.VMEM) for a in state))


def solution(mesh):
    return jax.shard_map(
        on_device,
        mesh=mesh,
        in_specs=(
            P(None, "gx", None, "gy"),
            P("gx", None, "gy"),
            P(None, "gx", None, "gy"),
            P("gx", None, "gy"),
        ),
        out_specs=(P(None, "gx", None, "gy"), P("gx", None, "gy")),
        check_vma=False,
    )
```

time: 40.5 us -> 36.6 us (0.904)
  Pallas kernels: 39.7 us -> 35.8 us
    pallas_call x1, Pallas kernels: 38.8 us -> 35 us  [on_device(): pl.pallas_call(kernel, out_shape=state_shape, in_specs=[hbm] * 4, out_spe...]
where the time goes in v3:
time: 36.6 us; the launch traced here: 36.5 us
  Pallas kernels  35.8 us (98%)
  between operations  0.64 us (2%)
    pallas_call x1, Pallas kernels, on_device(): pl.pallas_call(kernel, out_shape=state_shape, in_specs=[hbm] * 4, out_spe...  35 us
    pallas_call x1, Pallas kernels, on_device(): pl.pallas_call(write_back, out_shape=state_shape, in_specs=[here] * 2, ou...  0.85 us

profile of v3, /device:TPU:1, one launch (start us, length us, event | category | flops | bytes accessed | tf_op | source)
XLA Modules:
  0.0 36.5 jit_solution(17641231730798041288)
XLA Ops:
  0.6 35.0 %lattice_steps.1 = (f32[19,2,16,256]{3,2,1,0:T(8,128)S(1)}, f32[2,16,256]{2,1,0:T(8,128)S(1)}) custom-call(f32[19,2,16,256]{3,2,1,0:T(8,128)} %pops_in.1, f32[2,16,256]{2,1,0:T(8,128)} %mass_in.1, s32[2,2,16,256]{3,2,1,0:T(8,128)} %flags_in.1, f32[2,16,256]{2,1,0:T(8,128)} %relax_in.1), custom_call_target="tpu_custom_call" | custom-call | tf_op jit(solution)/shard_map/lattice_steps/pallas_call | solution.py:530
  35.6 0.8 %write_back.1 = (f32[19,2,16,256]{3,2,1,0:T(8,128)}, f32[2,16,256]{2,1,0:T(8,128)}) custom-call(f32[19,2,16,256]{3,2,1,0:T(8,128)S(1)} %get-tuple-element.4.pops, f32[2,16,256]{2,1,0:T(8,128)S(1)} %get-tuple-element.5.mass), custom_call_target="tpu_custom_call" | custom-call | tf_op jit(solution)/shard_map/write_back/pallas_call | solution.py:570

commit v4 on v3

--- a/solution.py
+++ b/solution.py
@@ -134,6 +134,9 @@
     ry,
     sk,
     rk,
+    held_x,
+    held_c,
+    held_k,
     load_sem,
     sx_sem,
     rx_sem,
@@ -143,21 +146,44 @@
     ry_sem,
     sk_sem,
     rk_sem,
+    held_x_sem,
+    held_c_sem,
+    held_k_sem,
+    on_sem,
+    go_sem,
 ):
     nx, ny = lax.axis_size("gx"), lax.axis_size("gy")
     gx, gy = lax.axis_index("gx"), lax.axis_index("gy")
     ys = [lax.rem(gy + ny - 1, ny), gy, lax.rem(gy + 1, ny)]
-    sides = [lax.rem(gx, 2), lax.rem(gx + 1, 2)]
+    parity = lax.rem(gx, 2)
+    sides = [parity, 1 - parity]
+    place = lax.rem(gx, 8)
+    early = (place == 0) | (place == 3)
+    late = (place == 4) | (place == 7)
+
+    def peer(dx, u):
+        return (lax.rem(gx + dx + nx, nx), ys[u + 1])
 
     def device(d, u):
-        return (lax.rem(gx + 2 * d - 1 + nx, nx), ys[u + 1])
+        return peer(2 * d - 1, u)
+
+    relay, relayed, beyond_relay = 2 * parity - 5, 3 + 2 * parity, 4
 
     barrier = pltpu.get_barrier_semaphore()
-    for d in sides:
-        for u in (0, -1, 1):
-            pl.semaphore_signal(barrier, inc=1, device_id=device(d, u), device_id_type=MESH)
-    for u in (-1, 1):
-        pl.semaphore_signal(barrier, inc=1, device_id=(gx, ys[u + 1]), device_id_type=MESH)
+
+    def greet(*devices):
+        for other in devices:
+            pl.semaphore_signal(barrier, inc=1, device_id=other, device_id_type=MESH)
+
+    @pl.when(jnp.logical_not(late))
+    def _():
+        greet(*[device(sides[0], u) for u in (0, -1, 1)])
+
+    @pl.when(early)
+    def _():
+        greet(peer(beyond_relay, 0), *[peer(relayed, u) for u in (0, -1, 1)])
+
+    greet(*[device(sides[1], u) for u in (0, -1, 1)], peer(0, -1), peer(0, 1))
     loads = [
         pltpu.make_async_copy(mass_in, mass.at[0], load_sem.at[0]),
         pltpu.make_async_copy(flags_in, flags, load_sem.at[1]),
@@ -196,6 +222,35 @@
     def y_tile(t, u, at):
         return pltpu.make_async_remote_copy(
             sy.at[t, u], ry.at[t, at], sy_sem.at[t, u], ry_sem.at[t, at], device_id=(gx, ys[2 * u]), device_id_type=MESH
+        )
+
+    def to_relay(src, dst, send, recv, u=0):
+        return pltpu.make_async_remote_copy(
+            src, dst, send, recv, device_id=peer(relay, u), device_id_type=MESH
+        )
+
+    def to_relay_corner(u):
+        d = parity
+        return to_relay(sk.at[0, d, u], held_k.at[1 - u], sk_sem.at[0, d, u], held_k_sem.at[1 - u], 2 * u - 1)
+
+    def to_relay_code():
+        return to_relay(sc.at[parity], held_c, sc_sem.at[parity], held_c_sem.at[0])
+
+    def to_relay_chunk(c):
+        d, count = parity, pl.ds(0, 5)
+        return to_relay(sx.at[0, d, c, count], held_x.at[c], sx_sem.at[0, d, c], held_x_sem.at[c])
+
+    def arrivals():
+        return [to_relay_corner(1), to_relay_corner(0), to_relay_code()] + [to_relay_chunk(c) for c in range(4)]
+
+    def onward(i):
+        d, count = parity, pl.ds(0, 5)
+        parts = [(held_k.at[u], rk.at[0, d, u], rk_sem.at[0, d, u]) for u in (0, 1)]
+        parts.append((held_c, rc.at[d], rc_sem.at[d]))
+        parts += [(held_x.at[c], rx.at[0, d, c, count], rx_sem.at[0, d, c]) for c in range(4)]
+        src, dst, recv = parts[i]
+        return pltpu.make_async_remote_copy(
+            src, dst, on_sem.at[i], recv, device_id=peer(beyond_relay, 0), device_id_type=MESH
         )
 
     def pick(pair, p):
@@ -239,16 +294,34 @@
     fill_y(0)
     loads[3].wait()
 
-    pl.semaphore_wait(barrier, 8)
-    for i, d in enumerate(sides):
+    pl.semaphore_wait(barrier, 8 + late.astype(jnp.int32))
+
+    @pl.when(late)
+    def _():
+        pl.semaphore_signal(go_sem, inc=1, device_id=peer(-beyond_relay, 0), device_id_type=MESH)
+
+    def open_side(d):
         for u in (0, 1):
             x_corner(0, d, u, (1 - d, 1 - u)).start()
         x_code(d, 1 - d).start()
         for c in range(4):
             x_chunk(0, d, c, 1 - d).start()
-        if i == 0:
-            for u in (0, 1):
-                y_tile(0, u, 1 - u).start()
+
+    @pl.when(early)
+    def _():
+        for u in (0, 1):
+            to_relay_corner(u).start()
+        to_relay_code().start()
+        for c in range(4):
+            to_relay_chunk(c).start()
+
+    @pl.when(jnp.logical_not(early))
+    def _():
+        open_side(sides[0])
+
+    for u in (0, 1):
+        y_tile(0, u, 1 - u).start()
+    open_side(sides[1])
 
     def stream(t):
         place = [{c: k for k, c in enumerate(y_columns(cy))} for cy in (1, -1)]
@@ -485,6 +558,15 @@
             y_tile(t, u, u).wait_recv()
         stream(t)
 
+        if t == 0:
+
+            @pl.when(early)
+            def _():
+                pl.semaphore_wait(go_sem, 1)
+                for i, arrival in enumerate(arrivals()):
+                    arrival.wait_recv()
+                    onward(i).start()
+
         @pl.loop(0, 2)
         def _(i, t=t):
             close(t, lax.rem(gx + 1 + i, 2))
@@ -493,6 +575,11 @@
             fill_y(1)
             for u in (0, 1):
                 y_tile(1, u, 1 - u).start()
+
+    @pl.when(early)
+    def _():
+        for i in range(7):
+            onward(i).wait_send()
 
     for d in (0, 1):
         x_code(d, 1 - d).wait_send()
@@ -551,6 +638,9 @@
             vmem((2, 2, *tile), f32),
             vmem((2, 2, 2, *tile), f32),
             vmem((2, 2, 2, *tile), f32),
+            vmem((4, 5, *tile), f32),
+            vmem(plane, f32),
+            vmem((2, *tile), f32),
             dma((4,)),
             dma((2, 2, 4)),
             dma((2, 2, 4)),
@@ -560,6 +650,11 @@
             dma((2, 2)),
             dma((2, 2, 2)),
             dma((2, 2, 2)),
+            dma((4,)),
+            dma((1,)),
+            dma((2,)),
+            dma((7,)),
+            pltpu.SemaphoreType.REGULAR,
         ],
         compiler_params=pltpu.CompilerParams(
             collective_id=0, has_side_effects=True, vmem_limit_bytes=32 * 1024 * 1024

time: 36.6 us -> 34.9 us (0.954)
  Pallas kernels: 35.8 us -> 34.1 us
    pallas_call x1, Pallas kernels: 35 us -> 33.2 us  [on_device(): pl.pallas_call(kernel, out_shape=state_shape, in_specs=[hbm] * 4, out_spe...]
where the time goes in v4:
time: 34.9 us; the launch traced here: 34.7 us
  Pallas kernels  34.1 us (98%)
  between operations  0.64 us (2%)
    pallas_call x1, Pallas kernels, on_device(): pl.pallas_call(kernel, out_shape=state_shape, in_specs=[hbm] * 4, out_spe...  33.2 us
    pallas_call x1, Pallas kernels, on_device(): pl.pallas_call(write_back, out_shape=state_shape, in_specs=[here] * 2, ou...  0.85 us

profile of v4, /device:TPU:1, one launch (start us, length us, event | category | flops | bytes accessed | tf_op | source)
XLA Modules:
  0.0 34.7 jit_solution(16255195230441918695)
XLA Ops:
  0.6 33.2 %lattice_steps.1 = (f32[19,2,16,256]{3,2,1,0:T(8,128)S(1)}, f32[2,16,256]{2,1,0:T(8,128)S(1)}) custom-call(f32[19,2,16,256]{3,2,1,0:T(8,128)} %pops_in.1, f32[2,16,256]{2,1,0:T(8,128)} %mass_in.1, s32[2,2,16,256]{3,2,1,0:T(8,128)} %flags_in.1, f32[2,16,256]{2,1,0:T(8,128)} %relax_in.1), custom_call_target="tpu_custom_call" | custom-call | tf_op jit(solution)/shard_map/lattice_steps/pallas_call | solution.py:617
  33.9 0.8 %write_back.1 = (f32[19,2,16,256]{3,2,1,0:T(8,128)}, f32[2,16,256]{2,1,0:T(8,128)}) custom-call(f32[19,2,16,256]{3,2,1,0:T(8,128)S(1)} %get-tuple-element.4.pops, f32[2,16,256]{2,1,0:T(8,128)S(1)} %get-tuple-element.5.mass), custom_call_target="tpu_custom_call" | custom-call | tf_op jit(solution)/shard_map/write_back/pallas_call | solution.py:665

commit v5 on v4

--- a/solution.py
+++ b/solution.py
@@ -169,21 +169,22 @@
 
     relay, relayed, beyond_relay = 2 * parity - 5, 3 + 2 * parity, 4
 
+    odd, last = lax.rem(gy, 2) == 1, gy == ny - 1
+    answers_up = late & odd & jnp.logical_not(last)
+    answers_down = late & (odd | (gy == 0))
     barrier = pltpu.get_barrier_semaphore()
 
-    def greet(*devices):
-        for other in devices:
-            pl.semaphore_signal(barrier, inc=1, device_id=other, device_id_type=MESH)
-
-    @pl.when(jnp.logical_not(late))
-    def _():
-        greet(*[device(sides[0], u) for u in (0, -1, 1)])
-
-    @pl.when(early)
-    def _():
-        greet(peer(beyond_relay, 0), *[peer(relayed, u) for u in (0, -1, 1)])
-
-    greet(*[device(sides[1], u) for u in (0, -1, 1)], peer(0, -1), peer(0, 1))
+    def greet(when, *devices):
+        @pl.when(when)
+        def _():
+            for other in devices:
+                pl.semaphore_signal(barrier, inc=1, device_id=other, device_id_type=MESH)
+
+    greet(jnp.logical_not(late), *[device(sides[0], u) for u in (0, -1, 1)])
+    greet(early, peer(beyond_relay, 0), *[peer(relayed, u) for u in (0, -1, 1)])
+    greet(jnp.logical_not(late) | answers_down, peer(0, -1))
+    greet(jnp.logical_not(late) | answers_up, peer(0, 1))
+    greet((place != 5) & (place != 6), *[device(sides[1], u) for u in (0, -1, 1)])
     loads = [
         pltpu.make_async_copy(mass_in, mass.at[0], load_sem.at[0]),
         pltpu.make_async_copy(flags_in, flags, load_sem.at[1]),
@@ -270,10 +271,9 @@
         for u in (0, 1):
             sy[t, u] = pack([rim_of(t, q, p, u) for q, p in y_columns(2 * u - 1)])
 
-    def fill_corner(t, p):
-        for u in (0, 1):
-            q = pick(outward[2 - u], p)
-            sk[t, p, u] = pack([rim_of(t, q, p, u), rim_of(t, None, p, u)])
+    def fill_corner(t, p, u):
+        q = pick(outward[2 - u], p)
+        sk[t, p, u] = pack([rim_of(t, q, p, u), rim_of(t, None, p, u)])
 
     loads[0].wait()
     loads[1].wait()
@@ -282,7 +282,8 @@
         sc[p] = code[0, p]
     loads[2].wait()
     for p in (0, 1):
-        fill_corner(0, p)
+        for u in (0, 1):
+            fill_corner(0, p, u)
         for k, (cy, cz) in enumerate(OFFS):
             halves = [pops[0, outward[k][p], p, :, half(h)] for h in (0, 1)]
             if cy:
@@ -294,7 +295,8 @@
     fill_y(0)
     loads[3].wait()
 
-    pl.semaphore_wait(barrier, 8 + late.astype(jnp.int32))
+    fewer = 2 * late.astype(jnp.int32) + answers_up.astype(jnp.int32) + answers_down.astype(jnp.int32)
+    pl.semaphore_wait(barrier, 8 - fewer)
 
     @pl.when(late)
     def _():
@@ -319,9 +321,15 @@
     def _():
         open_side(sides[0])
 
-    for u in (0, 1):
-        y_tile(0, u, 1 - u).start()
-    open_side(sides[1])
+    for u, answers in enumerate((answers_down, answers_up)):
+
+        @pl.when(jnp.logical_not(answers))
+        def _(u=u):
+            y_tile(0, u, 1 - u).start()
+
+    @pl.when(jnp.logical_not(late))
+    def _():
+        open_side(sides[1])
 
     def stream(t):
         place = [{c: k for k, c in enumerate(y_columns(cy))} for cy in (1, -1)]
@@ -508,6 +516,11 @@
             x_corner(t, p, u, (p, u)).wait_recv()
         if t == 0:
             x_code(p, p).wait_recv()
+
+            @pl.when(late & (p == sides[1]))
+            def _():
+                open_side(p)
+
             far_codes(0, p)
             for h in (0, 1):
                 interior(0, p, h, far[p, 0, :, half(h)])
@@ -524,14 +537,14 @@
                 for k in range(5):
                     sx[1, p, c, k] = new_out[k]
                 sx[1, p, c, 5] = code_new
-                x_chunk(1, p, c, 1 - p).start()
                 code[1, p, z, lanes] = code_new
-                mass[1, p, z, lanes] = mass_new
                 for q, value in new:
                     pops[1, q, p, z, lanes] = value
-            fill_corner(1, p)
-            for u in (0, 1):
-                x_corner(1, p, u, (1 - p, 1 - u)).start()
+                if c % 2 == 1:
+                    fill_corner(1, p, h)
+                    x_corner(1, p, h, (1 - p, 1 - h)).start()
+                x_chunk(1, p, c, 1 - p).start()
+                mass[1, p, z, lanes] = mass_new
             return
         for h in (0, 1):
             for z in (0, 1):
@@ -556,6 +569,14 @@
     for t in (0, 1):
         for u in (0, 1):
             y_tile(t, u, u).wait_recv()
+        if t == 0:
+
+            for u, answers in enumerate((answers_down, answers_up)):
+
+                @pl.when(answers)
+                def _(u=u):
+                    y_tile(0, u, 1 - u).start()
+
         stream(t)
 
         if t == 0:

time: 34.9 us -> 34.2 us (0.980)
  Pallas kernels: 34.1 us -> 33.4 us
    pallas_call x1, Pallas kernels: 33.2 us -> 32.6 us  [on_device(): pl.pallas_call(kernel, out_shape=state_shape, in_specs=[hbm] * 4, out_spe...]
where the time goes in v5:
time: 34.2 us; the launch traced here: 34 us
  Pallas kernels  33.4 us (98%)
  between operations  0.64 us (2%)
    pallas_call x1, Pallas kernels, on_device(): pl.pallas_call(kernel, out_shape=state_shape, in_specs=[hbm] * 4, out_spe...  32.6 us
    pallas_call x1, Pallas kernels, on_device(): pl.pallas_call(write_back, out_shape=state_shape, in_specs=[here] * 2, ou...  0.85 us

profile of v5, /device:TPU:1, one launch (start us, length us, event | category | flops | bytes accessed | tf_op | source)
XLA Modules:
  0.0 34.0 jit_solution(15798188700372319562)
XLA Ops:
  0.6 32.6 %lattice_steps.1 = (f32[19,2,16,256]{3,2,1,0:T(8,128)S(1)}, f32[2,16,256]{2,1,0:T(8,128)S(1)}) custom-call(f32[19,2,16,256]{3,2,1,0:T(8,128)} %pops_in.1, f32[2,16,256]{2,1,0:T(8,128)} %mass_in.1, s32[2,2,16,256]{3,2,1,0:T(8,128)} %flags_in.1, f32[2,16,256]{2,1,0:T(8,128)} %relax_in.1), custom_call_target="tpu_custom_call" | custom-call | tf_op jit(solution)/shard_map/lattice_steps/pallas_call | solution.py:638
  33.2 0.8 %write_back.1 = (f32[19,2,16,256]{3,2,1,0:T(8,128)}, f32[2,16,256]{2,1,0:T(8,128)}) custom-call(f32[19,2,16,256]{3,2,1,0:T(8,128)S(1)} %get-tuple-element.4.pops, f32[2,16,256]{2,1,0:T(8,128)S(1)} %get-tuple-element.5.mass), custom_call_target="tpu_custom_call" | custom-call | tf_op jit(solution)/shard_map/write_back/pallas_call | solution.py:686

commit v6 on v5

--- a/solution.py
+++ b/solution.py
@@ -170,8 +170,9 @@
     relay, relayed, beyond_relay = 2 * parity - 5, 3 + 2 * parity, 4
 
     odd, last = lax.rem(gy, 2) == 1, gy == ny - 1
+    first = gy == 0
     answers_up = late & odd & jnp.logical_not(last)
-    answers_down = late & (odd | (gy == 0))
+    answers_down = late & (odd | first)
     barrier = pltpu.get_barrier_semaphore()
 
     def greet(when, *devices):
@@ -181,7 +182,8 @@
                 pl.semaphore_signal(barrier, inc=1, device_id=other, device_id_type=MESH)
 
     greet(jnp.logical_not(late), *[device(sides[0], u) for u in (0, -1, 1)])
-    greet(early, peer(beyond_relay, 0), *[peer(relayed, u) for u in (0, -1, 1)])
+    greet(early, peer(beyond_relay, 0), peer(relayed, 0), peer(relayed, -1))
+    greet(early & jnp.logical_not(last), peer(relayed, 1))
     greet(jnp.logical_not(late) | answers_down, peer(0, -1))
     greet(jnp.logical_not(late) | answers_up, peer(0, 1))
     greet((place != 5) & (place != 6), *[device(sides[1], u) for u in (0, -1, 1)])
@@ -193,6 +195,14 @@
     ]
     for load in loads:
         load.start()
+
+    fewer = 2 * late.astype(jnp.int32) + answers_up.astype(jnp.int32) + answers_down.astype(jnp.int32)
+    greeted = 8 - fewer - (early & first).astype(jnp.int32)
+
+    @pl.when(late)
+    def _():
+        pl.semaphore_wait(barrier, greeted)
+        pl.semaphore_signal(go_sem, inc=1, device_id=peer(-beyond_relay, 0), device_id_type=MESH)
 
     def x_code(d, at):
         return pltpu.make_async_remote_copy(
@@ -295,12 +305,9 @@
     fill_y(0)
     loads[3].wait()
 
-    fewer = 2 * late.astype(jnp.int32) + answers_up.astype(jnp.int32) + answers_down.astype(jnp.int32)
-    pl.semaphore_wait(barrier, 8 - fewer)
-
-    @pl.when(late)
+    @pl.when(jnp.logical_not(late))
     def _():
-        pl.semaphore_signal(go_sem, inc=1, device_id=peer(-beyond_relay, 0), device_id_type=MESH)
+        pl.semaphore_wait(barrier, greeted)
 
     def open_side(d):
         for u in (0, 1):
@@ -311,11 +318,14 @@
 
     @pl.when(early)
     def _():
-        for u in (0, 1):
-            to_relay_corner(u).start()
+        to_relay_corner(1).start()
         to_relay_code().start()
         for c in range(4):
             to_relay_chunk(c).start()
+
+    @pl.when(early & jnp.logical_not(first))
+    def _():
+        to_relay_corner(0).start()
 
     @pl.when(jnp.logical_not(early))
     def _():
@@ -512,18 +522,21 @@
         return mass_new, new, new_out
 
     def close(t, p):
-        for u in (0, 1):
-            x_corner(t, p, u, (p, u)).wait_recv()
+        def corners():
+            for u in (0, 1):
+                x_corner(t, p, u, (p, u)).wait_recv()
+
         if t == 0:
             x_code(p, p).wait_recv()
+            for h in (0, 1):
+                interior(0, p, h, rc[p, :, half(h)])
+            corners()
 
             @pl.when(late & (p == sides[1]))
             def _():
                 open_side(p)
 
             far_codes(0, p)
-            for h in (0, 1):
-                interior(0, p, h, far[p, 0, :, half(h)])
             for c, (z, h) in enumerate(CHUNKS):
                 x_chunk(0, p, c, p).wait_recv()
                 sources = [rx[0, p, c, k] for k in range(5)]
@@ -550,6 +563,7 @@
             for z in (0, 1):
                 x_chunk(1, p, 2 * h + z, p).wait_recv()
             interior(1, p, h, jnp.concatenate([rx[1, p, 2 * h, 5], rx[1, p, 2 * h + 1, 5]], axis=0))
+        corners()
         far_codes(1, p)
         beyond = []
         for k, (cy, cz) in enumerate(OFFS):
@@ -576,6 +590,11 @@
                 @pl.when(answers)
                 def _(u=u):
                     y_tile(0, u, 1 - u).start()
+
+        if t == 0:
+            @pl.when(early & first)
+            def _():
+                to_relay_corner(0).start()
 
         stream(t)
 

time: 34.2 us -> 33.9 us (level)
  no operation moved by 1% of the time
where the time goes in v6:
time: 33.9 us; the launch traced here: 33.8 us
  Pallas kernels  33.2 us (98%)
  between operations  0.64 us (2%)
    pallas_call x1, Pallas kernels, on_device(): pl.pallas_call(kernel, out_shape=state_shape, in_specs=[hbm] * 4, out_spe...  32.3 us
    pallas_call x1, Pallas kernels, on_device(): pl.pallas_call(write_back, out_shape=state_shape, in_specs=[here] * 2, ou...  0.85 us

profile of v6, /device:TPU:1, one launch (start us, length us, event | category | flops | bytes accessed | tf_op | source)
XLA Modules:
  0.0 33.8 jit_solution(16249158169697265646)
XLA Ops:
  0.6 32.3 %lattice_steps.1 = (f32[19,2,16,256]{3,2,1,0:T(8,128)S(1)}, f32[2,16,256]{2,1,0:T(8,128)S(1)}) custom-call(f32[19,2,16,256]{3,2,1,0:T(8,128)} %pops_in.1, f32[2,16,256]{2,1,0:T(8,128)} %mass_in.1, s32[2,2,16,256]{3,2,1,0:T(8,128)} %flags_in.1, f32[2,16,256]{2,1,0:T(8,128)} %relax_in.1), custom_call_target="tpu_custom_call" | custom-call | tf_op jit(solution)/shard_map/lattice_steps/pallas_call | solution.py:657
  32.9 0.8 %write_back.1 = (f32[19,2,16,256]{3,2,1,0:T(8,128)}, f32[2,16,256]{2,1,0:T(8,128)}) custom-call(f32[19,2,16,256]{3,2,1,0:T(8,128)S(1)} %get-tuple-element.4.pops, f32[2,16,256]{2,1,0:T(8,128)S(1)} %get-tuple-element.5.mass), custom_call_target="tpu_custom_call" | custom-call | tf_op jit(solution)/shard_map/write_back/pallas_call | solution.py:705

commit v7 on v6

--- a/solution.py
+++ b/solution.py
@@ -41,6 +41,7 @@
 
 OPP_OFFS = [0, 2, 1, 4, 3]
 CHUNKS = [(zh, h) for h in (0, 1) for zh in (0, 1)]
+ORDER = (2, 3, 0, 1)
 
 
 def side_dirs(cx):
@@ -252,13 +253,13 @@
         return to_relay(sx.at[0, d, c, count], held_x.at[c], sx_sem.at[0, d, c], held_x_sem.at[c])
 
     def arrivals():
-        return [to_relay_corner(1), to_relay_corner(0), to_relay_code()] + [to_relay_chunk(c) for c in range(4)]
+        return [to_relay_corner(1), to_relay_corner(0), to_relay_code()] + [to_relay_chunk(c) for c in ORDER]
 
     def onward(i):
         d, count = parity, pl.ds(0, 5)
         parts = [(held_k.at[u], rk.at[0, d, u], rk_sem.at[0, d, u]) for u in (0, 1)]
         parts.append((held_c, rc.at[d], rc_sem.at[d]))
-        parts += [(held_x.at[c], rx.at[0, d, c, count], rx_sem.at[0, d, c]) for c in range(4)]
+        parts += [(held_x.at[c], rx.at[0, d, c, count], rx_sem.at[0, d, c]) for c in ORDER]
         src, dst, recv = parts[i]
         return pltpu.make_async_remote_copy(
             src, dst, on_sem.at[i], recv, device_id=peer(beyond_relay, 0), device_id_type=MESH
@@ -313,19 +314,19 @@
         for u in (0, 1):
             x_corner(0, d, u, (1 - d, 1 - u)).start()
         x_code(d, 1 - d).start()
-        for c in range(4):
+        for c in ORDER:
             x_chunk(0, d, c, 1 - d).start()
+
+    @pl.when(early & jnp.logical_not(first))
+    def _():
+        to_relay_corner(0).start()
 
     @pl.when(early)
     def _():
         to_relay_corner(1).start()
         to_relay_code().start()
-        for c in range(4):
+        for c in ORDER:
             to_relay_chunk(c).start()
-
-    @pl.when(early & jnp.logical_not(first))
-    def _():
-        to_relay_corner(0).start()
 
     @pl.when(jnp.logical_not(early))
     def _():
@@ -537,7 +538,8 @@
                 open_side(p)
 
             far_codes(0, p)
-            for c, (z, h) in enumerate(CHUNKS):
+            for c in ORDER:
+                z, h = CHUNKS[c]
                 x_chunk(0, p, c, p).wait_recv()
                 sources = [rx[0, p, c, k] for k in range(5)]
                 lane = lax.broadcasted_iota(jnp.int32, sources[0].shape, 1)
@@ -559,7 +561,7 @@
                 x_chunk(1, p, c, 1 - p).start()
                 mass[1, p, z, lanes] = mass_new
             return
-        for h in (0, 1):
+        for h in (1, 0):
             for z in (0, 1):
                 x_chunk(1, p, 2 * h + z, p).wait_recv()
             interior(1, p, h, jnp.concatenate([rx[1, p, 2 * h, 5], rx[1, p, 2 * h + 1, 5]], axis=0))

time: 33.9 us -> 33.1 us (0.976)
  Pallas kernels: 33.2 us -> 32.3 us
    pallas_call x1, Pallas kernels: 32.3 us -> 31.5 us  [on_device(): pl.pallas_call(kernel, out_shape=state_shape, in_specs=[hbm] * 4, out_spe...]
where the time goes in v7:
time: 33.1 us; the launch traced here: 32.9 us
  Pallas kernels  32.3 us (98%)
  between operations  0.64 us (2%)
    pallas_call x1, Pallas kernels, on_device(): pl.pallas_call(kernel, out_shape=state_shape, in_specs=[hbm] * 4, out_spe...  31.5 us
    pallas_call x1, Pallas kernels, on_device(): pl.pallas_call(write_back, out_shape=state_shape, in_specs=[here] * 2, ou...  0.85 us

profile of v7, /device:TPU:1, one launch (start us, length us, event | category | flops | bytes accessed | tf_op | source)
XLA Modules:
  0.0 32.9 jit_solution(1867485219189778637)
XLA Ops:
  0.6 31.5 %lattice_steps.1 = (f32[19,2,16,256]{3,2,1,0:T(8,128)S(1)}, f32[2,16,256]{2,1,0:T(8,128)S(1)}) custom-call(f32[19,2,16,256]{3,2,1,0:T(8,128)} %pops_in.1, f32[2,16,256]{2,1,0:T(8,128)} %mass_in.1, s32[2,2,16,256]{3,2,1,0:T(8,128)} %flags_in.1, f32[2,16,256]{2,1,0:T(8,128)} %relax_in.1), custom_call_target="tpu_custom_call" | custom-call | tf_op jit(solution)/shard_map/lattice_steps/pallas_call | solution.py:659
  32.1 0.8 %write_back.1 = (f32[19,2,16,256]{3,2,1,0:T(8,128)}, f32[2,16,256]{2,1,0:T(8,128)}) custom-call(f32[19,2,16,256]{3,2,1,0:T(8,128)S(1)} %get-tuple-element.4.pops, f32[2,16,256]{2,1,0:T(8,128)S(1)} %get-tuple-element.5.mass), custom_call_target="tpu_custom_call" | custom-call | tf_op jit(solution)/shard_map/write_back/pallas_call | solution.py:707

commit v8 on v7

--- a/solution.py
+++ b/solution.py
@@ -558,8 +558,9 @@
                 if c % 2 == 1:
                     fill_corner(1, p, h)
                     x_corner(1, p, h, (1 - p, 1 - h)).start()
+                mass[1, p, z, lanes] = mass_new
+            for c in ORDER:
                 x_chunk(1, p, c, 1 - p).start()
-                mass[1, p, z, lanes] = mass_new
             return
         for h in (1, 0):
             for z in (0, 1):

time: 33.1 us -> 32.5 us (0.982)
  Pallas kernels: 32.3 us -> 31.7 us
    pallas_call x1, Pallas kernels: 31.5 us -> 30.9 us  [on_device(): pl.pallas_call(kernel, out_shape=state_shape, in_specs=[hbm] * 4, out_spe...]
where the time goes in v8:
time: 32.5 us; the launch traced here: 32.4 us
  Pallas kernels  31.7 us (98%)
  between operations  0.64 us (2%)
    pallas_call x1, Pallas kernels, on_device(): pl.pallas_call(kernel, out_shape=state_shape, in_specs=[hbm] * 4, out_spe...  30.9 us
    pallas_call x1, Pallas kernels, on_device(): pl.pallas_call(write_back, out_shape=state_shape, in_specs=[here] * 2, ou...  0.85 us

profile of v8, /device:TPU:1, one launch (start us, length us, event | category | flops | bytes accessed | tf_op | source)
XLA Modules:
  0.0 32.4 jit_solution(14679725836407260695)
XLA Ops:
  0.6 30.9 %lattice_steps.1 = (f32[19,2,16,256]{3,2,1,0:T(8,128)S(1)}, f32[2,16,256]{2,1,0:T(8,128)S(1)}) custom-call(f32[19,2,16,256]{3,2,1,0:T(8,128)} %pops_in.1, f32[2,16,256]{2,1,0:T(8,128)} %mass_in.1, s32[2,2,16,256]{3,2,1,0:T(8,128)} %flags_in.1, f32[2,16,256]{2,1,0:T(8,128)} %relax_in.1), custom_call_target="tpu_custom_call" | custom-call | tf_op jit(solution)/shard_map/lattice_steps/pallas_call | solution.py:660
  31.5 0.8 %write_back.1 = (f32[19,2,16,256]{3,2,1,0:T(8,128)}, f32[2,16,256]{2,1,0:T(8,128)}) custom-call(f32[19,2,16,256]{3,2,1,0:T(8,128)S(1)} %get-tuple-element.4.pops, f32[2,16,256]{2,1,0:T(8,128)S(1)} %get-tuple-element.5.mass), custom_call_target="tpu_custom_call" | custom-call | tf_op jit(solution)/shard_map/write_back/pallas_call | solution.py:708
